TPU v7x, 32 devices: a whole 2x2x4 slice. The times are simulated.
32 devices in a mesh: dp: 8 (over z, x), tensor: 4 (over y, core).
Axes of the slice: x: 2, y: 2, z: 4, core: 2. Of those that a mesh axis runs over, the one named last changes fastest.
Arguments:
- tokens: bfloat16 [8, 1024, 1024], P('dp', 'tensor'), may hold values from -6 to 6
- clip_counts: int32 [8], P('dp'), may hold values from 0 to 1, as said below
- cotangent: bfloat16 [8, 1024, 1024], P('dp', 'tensor'), may hold values from -6 to 6
- norm1_gain: bfloat16 [2, 1024], P(None, 'dp'), may hold values from 0.5 to 1.5
- norm1_shift: bfloat16 [2, 1024], P(None, 'dp'), may hold values from -1.25 to 1.25
- w_query: bfloat16 [2, 1024, 1024], P(None, 'dp', 'tensor'), may hold values from -0.1875 to 0.1875
- query_bias: bfloat16 [2, 1024], P(None, 'dp'), may hold values from -3 to 3
- w_key: bfloat16 [2, 1024, 1024], P(None, 'dp', 'tensor'), may hold values from -0.1875 to 0.1875
- w_value: bfloat16 [2, 1024, 1024], P(None, 'dp', 'tensor'), may hold values from -0.1875 to 0.1875
- value_bias: bfloat16 [2, 1024], P(None, 'dp'), may hold values from -3 to 3
- w_out: bfloat16 [2, 1024, 1024], P(None, 'dp', 'tensor'), may hold values from -3 to 3
- out_bias: bfloat16 [2, 1024], P(None, 'dp'), may hold values from -1.75 to 1.75
- norm2_gain: bfloat16 [2, 1024], P(None, 'dp'), may hold values from 0.5 to 1.5
- norm2_shift: bfloat16 [2, 1024], P(None, 'dp'), may hold values from -1.25 to 1.25
- w_up: bfloat16 [2, 1024, 4096], P(None, 'dp', 'tensor'), may hold values from -0.1875 to 0.1875
- up_bias: bfloat16 [2, 4096], P(None, 'dp'), may hold values from -3 to 3
- w_down: bfloat16 [2, 1024, 4096], P(None, 'dp', 'tensor'), may hold values from -0.09375 to 0.09375
- down_bias: bfloat16 [2, 1024], P(None, 'dp'), may hold values from -1.75 to 1.75
Outputs:
- mixed: bfloat16 [8, 1024, 1024], P('dp', 'tensor')
- tokens_grad: float32 [8, 1024, 1024], P('dp', 'tensor')
- grad_norm1_gain: float32 [2, 1024], P(None, 'dp')
- grad_norm1_shift: float32 [2, 1024], P(None, 'dp')
- grad_w_query: float32 [2, 1024, 1024], P(None, 'dp', 'tensor')
- grad_query_bias: float32 [2, 1024], P(None, 'dp')
- grad_w_key: float32 [2, 1024, 1024], P(None, 'dp', 'tensor')
- grad_w_value: float32 [2, 1024, 1024], P(None, 'dp', 'tensor')
- grad_value_bias: float32 [2, 1024], P(None, 'dp')
- grad_w_out: float32 [2, 1024, 1024], P(None, 'dp', 'tensor')
- grad_out_bias: float32 [2, 1024], P(None, 'dp')
- grad_norm2_gain: float32 [2, 1024], P(None, 'dp')
- grad_norm2_shift: float32 [2, 1024], P(None, 'dp')
- grad_w_up: float32 [2, 1024, 4096], P(None, 'dp', 'tensor')
- grad_up_bias: float32 [2, 4096], P(None, 'dp')
- grad_w_down: float32 [2, 1024, 4096], P(None, 'dp', 'tensor')
- grad_down_bias: float32 [2, 1024], P(None, 'dp')
Inputs may be any that keep to these rules, and one draw needn't show every extreme that they name: clip_counts holds each slot's number of clips; some slot holds one clip and some slot none in every draw.
All inputs are finite; a program needn't handle non-finite values.
Results may differ from a plain program's by a relative error of at most 0.017.
Values may be sent and summed in bfloat16 or wider, within the bound.
A program may use at most 192 MiB of HBM per device.

v0:
```python
from functools import partial

import jax
import jax.numpy as jnp
from jax import lax
from jax.sharding import PartitionSpec as P

HD = 64


norm_eps = 1e-06


def layer_norm(inputs, gain_vec, shift_vec):
    row_mean = jnp.mean(inputs, axis=-1, keepdims=True)
    centered = inputs - row_mean
    variance = jnp.mean(centered * centered, axis=-1, keepdims=True)
    return centered * lax.rsqrt(variance + norm_eps) * gain_vec + shift_vec


def plain_dot(left_rows, right_rows):
    return jnp.dot(left_rows, right_rows, preferred_element_type=jnp.float32)


def right_dot(left_rows, weight_mat):
    return lax.dot_general(
        left_rows, weight_mat, (((1,), (1,)), ((), ())), preferred_element_type=jnp.float32
    )


def rows_dot(left_rows, right_rows):
    return lax.dot_general(
        left_rows, right_rows, (((0,), (0,)), ((), ())), preferred_element_type=jnp.float32
    )


def own_part(vector, tensor_rank, part_width):
    return lax.dynamic_slice_in_dim(vector, tensor_rank * part_width, part_width, 0)


def place_part(part_vals, tensor_rank, full_length):
    return lax.dynamic_update_slice_in_dim(
        jnp.zeros((full_length,), jnp.float32), part_vals, tensor_rank * part_vals.shape[0], 0
    )


def attend_forward(queries, key_rows, value_rows):
    seq_len = queries.shape[0]
    head_count = queries.shape[1] // HD
    block_count = max(1, seq_len // 512)
    block_rows = seq_len // block_count
    scaling = HD ** (-0.5)
    key_heads = key_rows.reshape(seq_len, head_count, HD)
    value_heads = value_rows.reshape(seq_len, head_count, HD)

    def one_block(query_block):
        scores = (
            jnp.einsum("qhd,khd->hqk", query_block, key_heads, preferred_element_type=jnp.float32)
            * scaling
        )
        row_max = jnp.max(scores, axis=-1, keepdims=True)
        exp_scores = jnp.exp(scores - row_max)
        totals = jnp.sum(exp_scores, axis=-1, keepdims=True)
        probs_low = (exp_scores / totals).astype(jnp.bfloat16)
        mixed_rows = jnp.einsum(
            "hqk,khd->qhd", probs_low, value_heads, preferred_element_type=jnp.float32
        )
        return (
            mixed_rows.astype(jnp.bfloat16).reshape(block_rows, head_count * HD),
            (row_max + jnp.log(totals))[..., 0],
        )

    outputs, log_sums = lax.map(one_block, queries.reshape(block_count, block_rows, head_count, HD))
    return (outputs.reshape(seq_len, head_count * HD), log_sums)


def attend_backward(queries, key_rows, value_rows, log_sums, grad_out):
    seq_len = queries.shape[0]
    head_count = queries.shape[1] // HD
    block_count = max(1, seq_len // 512)
    block_rows = seq_len // block_count
    scaling = HD ** (-0.5)
    key_heads = key_rows.reshape(seq_len, head_count, HD)
    value_heads = value_rows.reshape(seq_len, head_count, HD)
    query_blocks = queries.reshape(block_count, block_rows, head_count, HD)
    grad_blocks = grad_out.reshape(block_count, block_rows, head_count, HD)

    def one_block(running, inputs):
        key_grad, value_grad = running
        query_block, grad_block, lse_block = inputs
        scores = (
            jnp.einsum("qhd,khd->hqk", query_block, key_heads, preferred_element_type=jnp.float32)
            * scaling
        )
        prob_rows = jnp.exp(scores - lse_block[..., None])
        probs_low = prob_rows.astype(jnp.bfloat16)
        value_grad = value_grad + jnp.einsum(
            "hqk,qhd->khd", probs_low, grad_block, preferred_element_type=jnp.float32
        )
        prob_grad = jnp.einsum(
            "qhd,khd->hqk", grad_block, value_heads, preferred_element_type=jnp.float32
        )
        row_dot = jnp.sum(prob_rows * prob_grad, axis=-1, keepdims=True)
        score_grad = (prob_rows * (prob_grad - row_dot)).astype(jnp.bfloat16)
        query_grad = (
            jnp.einsum("hqk,khd->qhd", score_grad, key_heads, preferred_element_type=jnp.float32)
            * scaling
        )
        key_grad = (
            key_grad
            + jnp.einsum(
                "hqk,qhd->khd", score_grad, query_block, preferred_element_type=jnp.float32
            )
            * scaling
        )
        return ((key_grad, value_grad), query_grad)

    zero_heads = jnp.zeros((seq_len, head_count, HD), jnp.float32)
    (key_grad, value_grad), query_grads = lax.scan(
        one_block, (zero_heads, zero_heads), (query_blocks, grad_blocks, log_sums)
    )
    return (
        query_grads.reshape(seq_len, head_count * HD),
        key_grad.reshape(seq_len, head_count * HD),
        value_grad.reshape(seq_len, head_count * HD),
    )


def unpack(weights):
    (
        gain_first,
        shift_first,
        query_mat,
        query_offset,
        key_mat,
        value_mat,
        value_offset,
        out_mat,
        out_offset,
        gain_second,
        shift_second,
        up_mat,
        up_offset,
        down_mat,
        down_offset,
    ) = weights
    vectors = [
        member.astype(jnp.float32)
        for member in (
            gain_first,
            shift_first,
            query_offset,
            value_offset,
            out_offset,
            gain_second,
            shift_second,
            up_offset,
            down_offset,
        )
    ]
    return ((query_mat, key_mat, value_mat, out_mat, up_mat, down_mat), vectors)


def forward_layer(residual, weights, tensor_rank):
    (query_mat, key_mat, value_mat, out_mat, up_mat, down_mat), vectors = unpack(weights)
    (
        gain_first,
        shift_first,
        query_offset,
        value_offset,
        out_offset,
        gain_second,
        shift_second,
        up_offset,
        down_offset,
    ) = vectors
    head_cols = query_mat.shape[1]
    hidden_cols = up_mat.shape[1]
    normed = layer_norm(residual, gain_first, shift_first).astype(jnp.bfloat16)
    normed_full = lax.all_gather(normed, "tensor", axis=0, tiled=True)
    queries = (
        plain_dot(normed_full, query_mat) + own_part(query_offset, tensor_rank, head_cols)
    ).astype(jnp.bfloat16)
    key_rows = plain_dot(normed_full, key_mat).astype(jnp.bfloat16)
    value_rows = (
        plain_dot(normed_full, value_mat) + own_part(value_offset, tensor_rank, head_cols)
    ).astype(jnp.bfloat16)
    attended, log_sums = attend_forward(queries, key_rows, value_rows)
    branch = lax.psum_scatter(
        right_dot(attended, out_mat).astype(jnp.bfloat16), "tensor", scatter_dimension=0, tiled=True
    ).astype(jnp.float32)
    middle = residual + branch + out_offset
    normed_two = layer_norm(middle, gain_second, shift_second).astype(jnp.bfloat16)
    normed_two_full = lax.all_gather(normed_two, "tensor", axis=0, tiled=True)
    pre_act = plain_dot(normed_two_full, up_mat) + own_part(up_offset, tensor_rank, hidden_cols)
    activated = jax.nn.gelu(pre_act, approximate=False).astype(jnp.bfloat16)
    output = (
        middle
        + lax.psum_scatter(
            right_dot(activated, down_mat).astype(jnp.bfloat16),
            "tensor",
            scatter_dimension=0,
            tiled=True,
        ).astype(jnp.float32)
        + down_offset
    )
    stored = (
        residual,
        normed_full,
        queries,
        key_rows,
        value_rows,
        attended,
        log_sums,
        middle,
        normed_two_full,
        pre_act,
        activated,
    )
    return (output, stored)


def backward_layer(upstream, weights, stored, tensor_rank):
    (query_mat, key_mat, value_mat, out_mat, up_mat, down_mat), vectors = unpack(weights)
    (
        gain_first,
        shift_first,
        query_offset,
        value_offset,
        out_offset,
        gain_second,
        shift_second,
        up_offset,
        down_offset,
    ) = vectors
    (
        residual,
        normed_full,
        queries,
        key_rows,
        value_rows,
        attended,
        log_sums,
        middle,
        normed_two_full,
        pre_act,
        activated,
    ) = stored
    model_width = gain_first.shape[0]
    hidden_total = up_offset.shape[0]
    grad_low = upstream.astype(jnp.bfloat16)
    down_offset_grad = jnp.sum(grad_low.astype(jnp.float32), axis=0)
    grad_full = lax.all_gather(grad_low, "tensor", axis=0, tiled=True)
    down_grad = rows_dot(grad_full, activated)
    act_grad = plain_dot(grad_full, down_mat)
    gelu_pull = jax.vjp(partial(jax.nn.gelu, approximate=False), pre_act)[1]
    pre_grad = gelu_pull(act_grad)[0].astype(jnp.bfloat16)
    up_offset_grad = place_part(
        jnp.sum(pre_grad.astype(jnp.float32), axis=0), tensor_rank, hidden_total
    )
    up_grad = rows_dot(normed_two_full, pre_grad)
    two_grad = lax.psum_scatter(
        right_dot(pre_grad, up_mat).astype(jnp.bfloat16), "tensor", scatter_dimension=0, tiled=True
    ).astype(jnp.float32)
    norm_pull = jax.vjp(layer_norm, middle, gain_second, shift_second)[1]
    mid_part, gain_second_grad, shift_second_grad = norm_pull(two_grad)
    mid_grad = upstream + mid_part
    mid_low = mid_grad.astype(jnp.bfloat16)
    out_offset_grad = jnp.sum(mid_low.astype(jnp.float32), axis=0)
    mid_full = lax.all_gather(mid_low, "tensor", axis=0, tiled=True)
    out_grad = rows_dot(mid_full, attended)
    attended_grad = plain_dot(mid_full, out_mat).astype(jnp.bfloat16)
    query_grad, key_grad, value_grad = attend_backward(
        queries, key_rows, value_rows, log_sums, attended_grad
    )
    query_low = query_grad.astype(jnp.bfloat16)
    key_low = key_grad.astype(jnp.bfloat16)
    value_low = value_grad.astype(jnp.bfloat16)
    query_offset_grad = place_part(
        jnp.sum(query_low.astype(jnp.float32), axis=0), tensor_rank, model_width
    )
    value_offset_grad = place_part(
        jnp.sum(value_low.astype(jnp.float32), axis=0), tensor_rank, model_width
    )
    query_mat_grad = rows_dot(normed_full, query_low)
    key_mat_grad = rows_dot(normed_full, key_low)
    value_mat_grad = rows_dot(normed_full, value_low)
    normed_grad = lax.psum_scatter(
        (
            right_dot(query_low, query_mat)
            + right_dot(key_low, key_mat)
            + right_dot(value_low, value_mat)
        ).astype(jnp.bfloat16),
        "tensor",
        scatter_dimension=0,
        tiled=True,
    ).astype(jnp.float32)
    first_pull = jax.vjp(layer_norm, residual, gain_first, shift_first)[1]
    res_part, gain_first_grad, shift_first_grad = first_pull(normed_grad)
    grad_in = mid_grad + res_part
    summed = (
        lax.psum(gain_first_grad.astype(jnp.bfloat16), "tensor").astype(jnp.float32),
        lax.psum(shift_first_grad.astype(jnp.bfloat16), "tensor").astype(jnp.float32),
        lax.psum(query_offset_grad.astype(jnp.bfloat16), "tensor").astype(jnp.float32),
        lax.psum(value_offset_grad.astype(jnp.bfloat16), "tensor").astype(jnp.float32),
        lax.psum(out_offset_grad.astype(jnp.bfloat16), "tensor").astype(jnp.float32),
        lax.psum(gain_second_grad.astype(jnp.bfloat16), "tensor").astype(jnp.float32),
        lax.psum(shift_second_grad.astype(jnp.bfloat16), "tensor").astype(jnp.float32),
        lax.psum(up_offset_grad.astype(jnp.bfloat16), "tensor").astype(jnp.float32),
        lax.psum(down_offset_grad.astype(jnp.bfloat16), "tensor").astype(jnp.float32),
    )
    layer_grads = (
        summed[0],
        summed[1],
        query_mat_grad,
        summed[2],
        key_mat_grad,
        value_mat_grad,
        summed[3],
        out_grad,
        summed[4],
        summed[5],
        summed[6],
        up_grad,
        summed[7],
        down_grad,
        summed[8],
    )
    return (grad_in, layer_grads)


def shards(
    tokens,
    clip_counts,
    cotangent,
    norm1_gain,
    norm1_shift,
    w_query,
    query_bias,
    w_key,
    w_value,
    value_bias,
    w_out,
    out_bias,
    norm2_gain,
    norm2_shift,
    w_up,
    up_bias,
    w_down,
    down_bias,
):
    tensor_rank = lax.axis_index("tensor")
    layer_count = w_query.shape[0]
    live_mask = clip_counts[0].astype(jnp.float32)
    residual = tokens[0].astype(jnp.float32)
    fetched = []
    kept_layers = []
    for layer_index in range(layer_count):
        weights = (
            lax.all_gather(norm1_gain[layer_index], "dp", axis=0, tiled=True),
            lax.all_gather(norm1_shift[layer_index], "dp", axis=0, tiled=True),
            lax.all_gather(w_query[layer_index], "dp", axis=0, tiled=True),
            lax.all_gather(query_bias[layer_index], "dp", axis=0, tiled=True),
            lax.all_gather(w_key[layer_index], "dp", axis=0, tiled=True),
            lax.all_gather(w_value[layer_index], "dp", axis=0, tiled=True),
            lax.all_gather(value_bias[layer_index], "dp", axis=0, tiled=True),
            lax.all_gather(w_out[layer_index], "dp", axis=0, tiled=True),
            lax.all_gather(out_bias[layer_index], "dp", axis=0, tiled=True),
            lax.all_gather(norm2_gain[layer_index], "dp", axis=0, tiled=True),
            lax.all_gather(norm2_shift[layer_index], "dp", axis=0, tiled=True),
            lax.all_gather(w_up[layer_index], "dp", axis=0, tiled=True),
            lax.all_gather(up_bias[layer_index], "dp", axis=0, tiled=True),
            lax.all_gather(w_down[layer_index], "dp", axis=0, tiled=True),
            lax.all_gather(down_bias[layer_index], "dp", axis=0, tiled=True),
        )
        fetched.append(weights)
        residual, stored = forward_layer(residual, weights, tensor_rank)
        kept_layers.append(stored)
    mixed = residual.astype(jnp.bfloat16)[None]
    upstream = cotangent[0].astype(jnp.float32) * live_mask
    collected = []
    for layer_index in reversed(range(layer_count)):
        weights = (
            lax.all_gather(norm1_gain[layer_index], "dp", axis=0, tiled=True),
            lax.all_gather(norm1_shift[layer_index], "dp", axis=0, tiled=True),
            lax.all_gather(w_query[layer_index], "dp", axis=0, tiled=True),
            lax.all_gather(query_bias[layer_index], "dp", axis=0, tiled=True),
            lax.all_gather(w_key[layer_index], "dp", axis=0, tiled=True),
            lax.all_gather(w_value[layer_index], "dp", axis=0, tiled=True),
            lax.all_gather(value_bias[layer_index], "dp", axis=0, tiled=True),
            lax.all_gather(w_out[layer_index], "dp", axis=0, tiled=True),
            lax.all_gather(out_bias[layer_index], "dp", axis=0, tiled=True),
            lax.all_gather(norm2_gain[layer_index], "dp", axis=0, tiled=True),
            lax.all_gather(norm2_shift[layer_index], "dp", axis=0, tiled=True),
            lax.all_gather(w_up[layer_index], "dp", axis=0, tiled=True),
            lax.all_gather(up_bias[layer_index], "dp", axis=0, tiled=True),
            lax.all_gather(w_down[layer_index], "dp", axis=0, tiled=True),
            lax.all_gather(down_bias[layer_index], "dp", axis=0, tiled=True),
        )
        upstream, layer_grads = backward_layer(
            upstream, weights, kept_layers[layer_index], tensor_rank
        )
        collected.append(layer_grads)
    ordered = collected[::-1]
    stacked = [
        jnp.stack([ordered[position][member] for position in range(layer_count)])
        for member in range(15)
    ]
    finals = (
        lax.psum_scatter(stacked[0], "dp", scatter_dimension=1, tiled=True),
        lax.psum_scatter(stacked[1], "dp", scatter_dimension=1, tiled=True),
        lax.psum_scatter(stacked[2], "dp", scatter_dimension=1, tiled=True),
        lax.psum_scatter(stacked[3], "dp", scatter_dimension=1, tiled=True),
        lax.psum_scatter(stacked[4], "dp", scatter_dimension=1, tiled=True),
        lax.psum_scatter(stacked[5], "dp", scatter_dimension=1, tiled=True),
        lax.psum_scatter(stacked[6], "dp", scatter_dimension=1, tiled=True),
        lax.psum_scatter(stacked[7], "dp", scatter_dimension=1, tiled=True),
        lax.psum_scatter(stacked[8], "dp", scatter_dimension=1, tiled=True),
        lax.psum_scatter(stacked[9], "dp", scatter_dimension=1, tiled=True),
        lax.psum_scatter(stacked[10], "dp", scatter_dimension=1, tiled=True),
        lax.psum_scatter(stacked[11], "dp", scatter_dimension=1, tiled=True),
        lax.psum_scatter(stacked[12], "dp", scatter_dimension=1, tiled=True),
        lax.psum_scatter(stacked[13], "dp", scatter_dimension=1, tiled=True),
        lax.psum_scatter(stacked[14], "dp", scatter_dimension=1, tiled=True),
    )
    return (
        mixed,
        upstream[None],
        finals[0],
        finals[1],
        finals[2],
        finals[3],
        finals[4],
        finals[5],
        finals[6],
        finals[7],
        finals[8],
        finals[9],
        finals[10],
        finals[11],
        finals[12],
        finals[13],
        finals[14],
    )


def solution(mesh):
    return jax.shard_map(
        shards,
        mesh=mesh,
        in_specs=(
            P("dp", "tensor", None),
            P("dp"),
            P("dp", "tensor", None),
            P(None, "dp"),
            P(None, "dp"),
            P(None, "dp", "tensor"),
            P(None, "dp"),
            P(None, "dp", "tensor"),
            P(None, "dp", "tensor"),
            P(None, "dp"),
            P(None, "dp", "tensor"),
            P(None, "dp"),
            P(None, "dp"),
            P(None, "dp"),
            P(None, "dp", "tensor"),
            P(None, "dp"),
            P(None, "dp", "tensor"),
            P(None, "dp"),
        ),
        out_specs=(
            P("dp", "tensor", None),
            P("dp", "tensor", None),
            P(None, "dp"),
            P(None, "dp"),
            P(None, "dp", "tensor"),
            P(None, "dp"),
            P(None, "dp", "tensor"),
            P(None, "dp", "tensor"),
            P(None, "dp"),
            P(None, "dp", "tensor"),
            P(None, "dp"),
            P(None, "dp"),
            P(None, "dp"),
            P(None, "dp", "tensor"),
            P(None, "dp"),
            P(None, "dp", "tensor"),
            P(None, "dp"),
        ),
        check_vma=False,
    )
```

profile of v0, /device:TPU:0, one launch (start us, length us, event | category | flops | bytes accessed | tf_op | source)
XLA Modules:
  0.0 2351.5 jit_solution(18038539800478347520)
XLA Ops:
  91.9 31.6 %all-gather.2 = bf16[1,1024,256]{2,1,0:T(8,128)(2,1)S(1)} all-gather(bf16[1,128,256]{2,1,0:T(8,128)(2,1)S(1)} %get-tuple-element.472), channel_id=4, replica_groups=mesh['dp'=8,'tensor'=4] {'dp'}, dimensions={1}, use_global_device_ids=true | all-gather | bytes 589824 | tf_op jit(solution)/shard_map/all_gather | solution.py:362
  123.6 31.5 %all-gather.5 = bf16[1,1024,256]{2,1,0:T(8,128)(2,1)S(1)} all-gather(bf16[1,128,256]{2,1,0:T(8,128)(2,1)S(1)} %get-tuple-element.468), channel_id=7, replica_groups=mesh['dp'=8,'tensor'=4] {'dp'}, dimensions={1}, use_global_device_ids=true | all-gather | bytes 589824 | tf_op jit(solution)/shard_map/all_gather | solution.py:365
  469.8 31.5 %all-gather.17 = bf16[1,1024,256]{2,1,0:T(8,128)(2,1)S(1)} all-gather(bf16[1,128,256]{2,1,0:T(8,128)(2,1)S(1)} %get-tuple-element.471), channel_id=19, replica_groups=mesh['dp'=8,'tensor'=4] {'dp'}, dimensions={1}, use_global_device_ids=true | all-gather | bytes 589824 | tf_op jit(solution)/shard_map/all_gather | solution.py:362
  501.3 33.5 %all-gather.20 = bf16[1,1024,256]{2,1,0:T(8,128)(2,1)} all-gather(bf16[1,128,256]{2,1,0:T(8,128)(2,1)S(1)} %get-tuple-element.467), channel_id=22, replica_groups=mesh['dp'=8,'tensor'=4] {'dp'}, dimensions={1}, use_global_device_ids=true | all-gather | bytes 589824 | tf_op jit(solution)/shard_map/all_gather | solution.py:365
  534.8 33.4 %all-gather.19 = bf16[1,1024,256]{2,1,0:T(8,128)(2,1)} all-gather(bf16[1,128,256]{2,1,0:T(8,128)(2,1)S(1)} %get-tuple-element.469), channel_id=21, replica_groups=mesh['dp'=8,'tensor'=4] {'dp'}, dimensions={1}, use_global_device_ids=true | all-gather | bytes 589824 | tf_op jit(solution)/shard_map/all_gather | solution.py:364
  568.2 33.6 %all-gather.22 = bf16[1,1024,256]{2,1,0:T(8,128)(2,1)} all-gather(bf16[1,128,256]{2,1,0:T(8,128)(2,1)S(1)} %get-tuple-element.465), channel_id=24, replica_groups=mesh['dp'=8,'tensor'=4] {'dp'}, dimensions={1}, use_global_device_ids=true | all-gather | bytes 589824 | tf_op jit(solution)/shard_map/all_gather | solution.py:367
  727.3 52.2 %all-gather.65.cloned.1.call-done = bf16[1,1024,1024]{2,1,0:T(8,128)(2,1)} async-done(((bf16[1,128,1024]{2,1,0:T(8,128)(2,1)}), bf16[1,1024,1024]{2,1,0:T(8,128)(2,1)}) %all-gather.65.cloned.1.call-update) | async-done | bytes 2097168 | tf_op jit(solution)/shard_map/all_gather | solution.py:373
  825.7 31.8 %reduce-scatter.48.cloned.1.call-done = bf16[256,1024]{1,0:T(8,128)(2,1)} async-done(((bf16[1024,1024]{1,0:T(8,128)(2,1)}), bf16[256,1024]{1,0:T(8,128)(2,1)}) %reduce-scatter.48.cloned.1.call-update) | async-done | bytes 524304 | tf_op jit(solution)/shard_map/reduce_scatter | solution.py:199
  891.4 38.1 %while.56 = (s32[]{:T(128)}, f32[1024,4,64]{0,2,1:T(8,128)S(1)}, f32[1024,4,64]{0,2,1:T(8,128)}, bf16[2,512,4,64]{1,3,2,0:T(8,128)(2,1)}, bf16[2,512,4,64]{1,3,2...) while((s32[]{:T(128)}, f32[1024,4,64]{0,2,1:T(8,128)S(1)}, ...), condition=%wide.region_25.26_spmd.clone, body=%wide.region_23.25_spmd.clone.sunk | while | flops 1368782848 | bytes 137421520 | solution.py:119
  1081.0 39.1 %while.57 = (s32[]{:T(128)}, f32[1024,4,64]{0,2,1:T(8,128)S(1)}, f32[1024,4,64]{0,2,1:T(8,128)S(1)}, bf16[2,512,4,64]{1,3,2,0:T(8,128)(2,1)}, bf16[2,512,4,64]{1...) while((s32[]{:T(128)}, f32[1024,4,64]{0,2,1:T(8,128)S(1)}, ...), condition=%wide.region_34.35_spmd.clone, body=%wide.region_32.34_spmd.clone.sunk | while | flops 1368782848 | bytes 147907920 | solution.py:119
  1239.7 63.1 %reduce-scatter.86.cloned.1.call-done = f32[128,2]{1,0:T(8,128)} async-done(((f32[1024,2]{1,0:T(8,128)}), f32[128,2]{1,0:T(8,128)}) %reduce-scatter.86.cloned.1.call-update) | async-done | bytes 1040
  1304.3 62.9 %reduce-scatter.78.cloned.1.call-done = f32[128,2]{1,0:T(8,128)} async-done(((f32[1024,2]{1,0:T(8,128)}), f32[128,2]{1,0:T(8,128)}) %reduce-scatter.78.cloned.1.call-update) | async-done | bytes 1040
  1368.7 63.3 %reduce-scatter.80.cloned.1.call-done = f32[128,2]{1,0:T(8,128)} async-done(((f32[1024,2]{1,0:T(8,128)}), f32[128,2]{1,0:T(8,128)}) %reduce-scatter.80.cloned.1.call-update) | async-done | bytes 1040
  1433.5 63.0 %reduce-scatter.74.cloned.1.call-done = f32[128,2]{1,0:T(8,128)} async-done(((f32[1024,2]{1,0:T(8,128)}), f32[128,2]{1,0:T(8,128)}) %reduce-scatter.74.cloned.1.call-update) | async-done | bytes 1040
  1497.9 63.3 %reduce-scatter.76.cloned.1.call-done = f32[128,2]{1,0:T(8,128)} async-done(((f32[1024,2]{1,0:T(8,128)}), f32[128,2]{1,0:T(8,128)}) %reduce-scatter.76.cloned.1.call-update) | async-done | bytes 1040
  1562.7 62.9 %reduce-scatter.70.cloned.1.call-done = f32[128,2]{1,0:T(8,128)} async-done(((f32[1024,2]{1,0:T(8,128)}), f32[128,2]{1,0:T(8,128)}) %reduce-scatter.70.cloned.1.call-update) | async-done | bytes 1040
  1627.1 63.2 %reduce-scatter.72.cloned.1.call-done = f32[128,2]{1,0:T(8,128)} async-done(((f32[1024,2]{1,0:T(8,128)}), f32[128,2]{1,0:T(8,128)}) %reduce-scatter.72.cloned.1.call-update) | async-done | bytes 1040
  1691.7 68.9 %reduce-scatter.84.cloned.1.call-done = f32[512,2]{1,0:T(8,128)} async-done(((f32[4096,2]{1,0:T(8,128)}), f32[512,2]{1,0:T(8,128)}) %reduce-scatter.84.cloned.1.call-update) | async-done | bytes 4112
  1762.3 68.9 %reduce-scatter.64.cloned.1.call-done = f32[2,128,256]{2,1,0:T(8,128)} async-done(((f32[2,1024,256]{2,1,0:T(8,128)}), f32[2,128,256]{2,1,0:T(8,128)}) %reduce-scatter.64.cloned.1.call-update) | async-done | bytes 262160 | tf_op jit(solution)/shard_map/reduce_scatter | solution.py:417
  1831.1 70.4 %reduce-scatter.62.cloned.1.call-done = f32[2,128,256]{2,1,0:T(8,128)} async-done(((f32[2,1024,256]{2,1,0:T(8,128)}), f32[2,128,256]{2,1,0:T(8,128)}) %reduce-scatter.62.cloned.1.call-update) | async-done | bytes 262160 | tf_op jit(solution)/shard_map/reduce_scatter | solution.py:415
  1901.5 70.5 %reduce-scatter.60.cloned.1.call-done = f32[2,128,256]{2,1,0:T(8,128)} async-done(((f32[2,1024,256]{2,1,0:T(8,128)}), f32[2,128,256]{2,1,0:T(8,128)}) %reduce-scatter.60.cloned.1.call-update) | async-done | bytes 262160 | tf_op jit(solution)/shard_map/reduce_scatter | solution.py:414
  1972.1 70.7 %reduce-scatter.58.cloned.1.call-done = f32[2,128,256]{2,1,0:T(8,128)} async-done(((f32[2,1024,256]{2,1,0:T(8,128)}), f32[2,128,256]{2,1,0:T(8,128)}) %reduce-scatter.58.cloned.1.call-update) | async-done | bytes 262160 | tf_op jit(solution)/shard_map/reduce_scatter | solution.py:412
  2042.7 150.1 %reduce-scatter.68.cloned.1.call-done = f32[2,128,1024]{2,1,0:T(8,128)} async-done(((f32[2,1024,1024]{2,1,0:T(8,128)}), f32[2,128,1024]{2,1,0:T(8,128)}) %reduce-scatter.68.cloned.1.call-update) | async-done | bytes 1048592 | tf_op jit(solution)/shard_map/reduce_scatter | solution.py:423
  2192.9 150.8 %reduce-scatter.66.cloned.1.call-done = f32[2,128,1024]{2,1,0:T(8,128)} async-done(((f32[2,1024,1024]{2,1,0:T(8,128)}), f32[2,128,1024]{2,1,0:T(8,128)}) %reduce-scatter.66.cloned.1.call-update) | async-done | bytes 1048592 | tf_op jit(solution)/shard_map/reduce_scatter | solution.py:421
  (607 shorter events, 987.8 us)
Async XLA Ops:
  8.0 209.7 %all-gather.43.cloned.1.call-start = ((), (), s32[]{:S(2)}) async-start(), calls=%async_computation.23 | async-start | bytes 2621440 | tf_op jit(solution)/shard_map/all_gather | solution.py:180
  52.5 244.7 %reduce-scatter.42.cloned.1.call-start = ((), (), s32[]{:S(2)}) async-start(), calls=%async_computation.24 | async-start | bytes 2621440 | tf_op jit(solution)/shard_map/reduce_scatter | solution.py:189
  303.1 129.5 %reduce-scatter.44.cloned.1.call-start = ((), (), s32[]{:S(2)}) async-start(), calls=%async_computation.26 | async-start | bytes 2621440 | tf_op jit(solution)/shard_map/reduce_scatter | solution.py:199
  380.3 221.5 %all-gather.47.cloned.1.call-start = ((), (), s32[]{:S(2)}) async-start(), calls=%async_computation.27 | async-start | bytes 2621440 | tf_op jit(solution)/shard_map/all_gather | solution.py:180
  435.4 242.8 %reduce-scatter.46.cloned.1.call-start = ((), (), s32[]{:S(2)}) async-start(), calls=%async_computation.28 | async-start | bytes 2621440 | tf_op jit(solution)/shard_map/reduce_scatter | solution.py:189
  683.8 95.7 %all-gather.65.cloned.1.call-start = ((), (), s32[]{:S(2)}) async-start(), calls=%async_computation.48 | async-start | bytes 2359296 | tf_op jit(solution)/shard_map/all_gather | solution.py:373
  684.3 139.3 %reduce-scatter.50.cloned.1.call-start = ((), (), s32[]{:S(2)}) async-start(), calls=%async_computation.32 | async-start | bytes 2621440 | tf_op jit(solution)/shard_map/reduce_scatter | solution.py:262
  862.5 107.4 %reduce-scatter.52.cloned.1.call-start = ((), (), s32[]{:S(2)}) async-start(), calls=%async_computation.34 | async-start | bytes 2621440 | tf_op jit(solution)/shard_map/reduce_scatter | solution.py:288
  1049.4 108.8 %reduce-scatter.56.cloned.1.call-start = ((), (), s32[]{:S(2)}) async-start(), calls=%async_computation.38 | async-start | bytes 2621440 | tf_op jit(solution)/shard_map/reduce_scatter | solution.py:288
  1126.7 111.5 %reduce-scatter.82.cloned.1.call-start = ((), (), s32[]{:S(2)}) async-start(), calls=%async_computation.55 | async-start | bytes 589824
  1174.9 127.9 %reduce-scatter.86.cloned.1.call-start = ((), (), s32[]{:S(2)}) async-start(), calls=%async_computation.57 | async-start | bytes 589824
  1176.0 191.2 %reduce-scatter.78.cloned.1.call-start = ((), (), s32[]{:S(2)}) async-start(), calls=%async_computation.53 | async-start | bytes 589824
  1177.2 254.9 %reduce-scatter.80.cloned.1.call-start = ((), (), s32[]{:S(2)}) async-start(), calls=%async_computation.54 | async-start | bytes 589824
  1178.3 318.2 %reduce-scatter.74.cloned.1.call-start = ((), (), s32[]{:S(2)}) async-start(), calls=%async_computation.51 | async-start | bytes 589824
  1179.4 381.8 %reduce-scatter.76.cloned.1.call-start = ((), (), s32[]{:S(2)}) async-start(), calls=%async_computation.52 | async-start | bytes 589824
  1183.9 441.7 %reduce-scatter.70.cloned.1.call-start = ((), (), s32[]{:S(2)}) async-start(), calls=%async_computation.49 | async-start | bytes 589824
  1185.1 505.1 %reduce-scatter.72.cloned.1.call-start = ((), (), s32[]{:S(2)}) async-start(), calls=%async_computation.50 | async-start | bytes 589824
  1189.6 571.0 %reduce-scatter.84.cloned.1.call-start = ((), (), s32[]{:S(2)}) async-start(), calls=%async_computation.56 | async-start | bytes 2359296
  1191.7 639.5 %reduce-scatter.64.cloned.1.call-start = ((), (), s32[]{:S(2)}) async-start(), calls=%async_computation.42 | async-start | bytes 2359296 | tf_op jit(solution)/shard_map/reduce_scatter | solution.py:417
  1194.5 707.0 %reduce-scatter.62.cloned.1.call-start = ((), (), s32[]{:S(2)}) async-start(), calls=%async_computation.41 | async-start | bytes 2359296 | tf_op jit(solution)/shard_map/reduce_scatter | solution.py:415
  1199.4 772.6 %reduce-scatter.60.cloned.1.call-start = ((), (), s32[]{:S(2)}) async-start(), calls=%async_computation.40 | async-start | bytes 2359296 | tf_op jit(solution)/shard_map/reduce_scatter | solution.py:414
  1204.3 838.4 %reduce-scatter.58.cloned.1.call-start = ((), (), s32[]{:S(2)}) async-start(), calls=%async_computation.39 | async-start | bytes 2359296 | tf_op jit(solution)/shard_map/reduce_scatter | solution.py:412
  1209.5 983.4 %reduce-scatter.68.cloned.1.call-start = ((), (), s32[]{:S(2)}) async-start(), calls=%async_computation.44 | async-start | bytes 9437184 | tf_op jit(solution)/shard_map/reduce_scatter | solution.py:423
  1221.1 1122.6 %reduce-scatter.66.cloned.1.call-start = ((), (), s32[]{:S(2)}) async-start(), calls=%async_computation.43 | async-start | bytes 9437184 | tf_op jit(solution)/shard_map/reduce_scatter | solution.py:421
  (131 other events, 4096.0 us)
Sparse Core Ops, SparseCore 0:
  52.7 21.3 all-gather.42
  243.8 29.9 reduce-scatter.41
  380.4 29.9 reduce-scatter.43
  626.8 28.6 reduce-scatter.45
  793.7 29.9 reduce-scatter.49
  826.0 31.4 reduce-scatter.47
  862.6 22.5 all-gather.52
  975.8 22.5 all-gather.54
  1012.1 31.4 reduce-scatter.53
Sparse Core Ops, SparseCore 1:
  247.1 47.7 all-gather.58
  324.9 49.3 all-gather.60
  630.4 46.5 all-gather.62
  681.6 21.1 all-gather.48
  704.8 22.4 all-gather.50
  730.1 49.3 all-gather.64
  938.5 31.3 reduce-scatter.51
  1049.4 22.4 all-gather.56
  1126.8 31.3 reduce-scatter.55
  1175.0 63.1 reduce-scatter.81
  1241.8 61.0 reduce-scatter.85
  1306.2 61.0 reduce-scatter.77
  1370.9 61.0 reduce-scatter.79
  1435.4 61.0 reduce-scatter.73
  1500.2 61.0 reduce-scatter.75
  1564.6 61.0 reduce-scatter.69
  1629.2 61.0 reduce-scatter.71
  1693.8 66.8 reduce-scatter.83
  1764.6 66.5 reduce-scatter.63
  1835.1 66.4 reduce-scatter.61
  1905.5 66.5 reduce-scatter.59
  1976.2 66.5 reduce-scatter.57
  2046.8 146.0 reduce-scatter.67
  2197.5 146.1 reduce-scatter.65
  (2 shorter events, 39.4 us)
where the time goes:
time: 2360 us; the launch traced here: 2350 us
  waiting for transfers between devices  1370 us (58%)
  blocking collectives  602 us (26%)
  matrix products  209 us (9%)
  other arithmetic  80.1 us (3%)
  local copies, waits for them, and re-layouts  63.6 us (3%)
    unnamed x44, waiting for transfers between devices  514 us
    reduce_scatter x1, waiting for transfers between devices, shards(): lax.psum_scatter(stacked[11], 'dp', scatter_dimension=1, tiled=True)  151 us
    reduce_scatter x1, waiting for transfers between devices, shards(): lax.psum_scatter(stacked[13], 'dp', scatter_dimension=1, tiled=True)  150 us
    all_gather x2, waiting for transfers between devices, shards(): lax.all_gather(w_down[layer_index], 'dp', axis=0, tiled=True)  81.9 us
    reduce_scatter x1, waiting for transfers between devices, shards(): lax.psum_scatter(stacked[2], 'dp', scatter_dimension=1, tiled=True)  70.7 us
    reduce_scatter x1, waiting for transfers between devices, shards(): lax.psum_scatter(stacked[4], 'dp', scatter_dimension=1, tiled=True)  70.5 us
    reduce_scatter x1, waiting for transfers between devices, shards(): lax.psum_scatter(stacked[5], 'dp', scatter_dimension=1, tiled=True)  70.4 us
    reduce_scatter x1, waiting for transfers between devices, shards(): lax.psum_scatter(stacked[7], 'dp', scatter_dimension=1, tiled=True)  68.9 us
  transfers between devices with their start and end apart: 35, of which 26 were waited for; matrix products, arithmetic and copies ran while one was open for 5% of the time, Pallas kernels for 0%

commit v1 on v0

v1 whole, which is shorter than its diff:
```python
import functools
import math

import jax
import jax.numpy as jnp
from jax import lax
from jax.experimental import pallas as pl
from jax.experimental.pallas import tpu as pltpu
from jax.sharding import PartitionSpec as P

HD = 64
norm_eps = 1e-06
MESH = pl.DeviceIdType.MESH
bf16 = jnp.bfloat16
f32 = jnp.float32
ROOT_HALF = 1.0 / math.sqrt(2.0)
PHI_ZERO = 1.0 / math.sqrt(2.0 * math.pi)
LOG2E = 1.0 / math.log(2.0)
CHUNK = 64


def dot_nn(left, right):
    return jnp.dot(left, right, preferred_element_type=f32)


def dot_nt(left, right):
    return lax.dot_general(left, right, (((1,), (1,)), ((), ())), preferred_element_type=f32)


def dot_tn(left, right):
    return lax.dot_general(left, right, (((0,), (0,)), ((), ())), preferred_element_type=f32)


def repeat(low, high, body):
    if high - low <= 4:
        for index in range(low, high):
            body(index)
    else:

        @pl.loop(low, high)
        def _(index):
            body(index)


def norm_parts(rows):
    centered = rows - jnp.mean(rows, axis=-1, keepdims=True)
    scale = lax.rsqrt(jnp.mean(centered * centered, axis=-1, keepdims=True) + norm_eps)
    return centered * scale, scale


def encoder_kernel(
    dims,
    tok, cot, counts, wq, wk, wv, wo, wu, wd, vec,
    mixed, tgrad, gq, gk, gv, go, gu, gd, vg, spill,
    W, NF, QKV, AT, LSE, X, MID, NF2, ACT, GP, GF, MF, DQKV, DO, GC, BR, AR,
    SA, SB, SC, RA, RB, RC, ACC, OST, VT, KT, DKA, DVA, STB,
    loc, ag_s, ag_r, rs_s, rs_r, wz_s, wz_r, wx_s, wx_r, gb_s, gb_r, ga_s, ga_r, cred_b, cred_a,
):
    A, B, S, R, D, HC, FC = dims
    heads = HC // HD
    score_scale = HD ** (-0.5)
    dp = lax.axis_index("dp")
    t = lax.axis_index("tensor")
    a = dp // B
    b = dp % B
    y = t // 2
    c = t % 2

    def flip(i):
        return 2 * ((y + i // 2) % 2) + (c + i % 2) % 2

    sib = (dp, flip(1))
    ypeer = (dp, flip(2))

    def dp_dev(aa, bb):
        return (aa * B + bb, t)

    def far(k):
        return (a + k) % A

    def near(j):
        return (b + j) % B

    groups = ((0, 3 * HC), (3 * HC, HC), (4 * HC, FC), (4 * HC + FC, FC))

    def blk(i):
        return pl.ds(pl.multiple_of(i * R, R), R)

    def shard(aa, bb):
        return pl.ds(pl.multiple_of((aa * B + bb) * S, S), S)

    def remote(src, dst, send, recv, device):
        return pltpu.make_async_remote_copy(
            src_ref=src, dst_ref=dst, send_sem=send, recv_sem=recv, device_id=device, device_id_type=MESH
        )

    barrier = pltpu.get_barrier_semaphore()

    def greet(device):
        pl.semaphore_signal(barrier, inc=1, device_id=device, device_id_type=MESH)

    greet(sib)
    greet(ypeer)
    repeat(1, A, lambda k: greet(dp_dev(far(k), b)))
    repeat(1, B, lambda j: greet(dp_dev(a, near(j))))

    def load_weight(l, g):
        parts = {
            0: ((wq, 0, HC), (wk, HC, HC), (wv, 2 * HC, HC)),
            1: ((wo, 3 * HC, HC),),
            2: ((wu, 4 * HC, FC),),
            3: ((wd, 4 * HC + FC, FC),),
        }[g]
        return [
            pltpu.make_async_copy(
                src.at[l], W.at[l, shard(a, b), pl.ds(first, width)], loc.at[l, 2 * g + place if g == 0 else g + 2]
            )
            for place, (src, first, width) in enumerate(parts)
        ]

    for l in range(2):
        for g in range(4):
            for copy in load_weight(l, g):
                copy.start()
    tok_copy = pltpu.make_async_copy(tok.at[0], STB, loc.at[0, 6])
    tok_copy.start()
    pl.semaphore_wait(barrier, A + B)

    def wrow(l, aa, bb, g):
        return W.at[l, shard(aa, bb), pl.ds(groups[g][0], groups[g][1])]

    def wz(l, g, k, source, device):
        ref = wrow(l, source, b, g)
        return remote(ref, ref, wz_s.at[l, g, k], wz_r.at[l, g, k], device)

    def wx(l, g, k, j, minor, device):
        ref = wrow(l, (a - k + A) % A, minor, g)
        return remote(ref, ref, wx_s.at[l, g, k, j], wx_r.at[l, g, k, j], device)

    def w_send_x(l, g, k):
        repeat(1, B, lambda j: wx(l, g, k, j, b, dp_dev(a, near(j))).start())

    def w_start(l, g):
        for copy in load_weight(l, g):
            copy.wait()
        repeat(1, A, lambda k: wz(l, g, k, a, dp_dev(far(k), b)).start())
        w_send_x(l, g, 0)

    def w_pump(l, g):
        def one(k):
            wz(l, g, k, (a - k + A) % A, dp_dev(far(k), b)).wait_recv()
            w_send_x(l, g, k)

        repeat(1, A, one)

    def w_done(l, g):
        def one(k):
            repeat(1, B, lambda j: wx(l, g, k, j, (b - j + B) % B, dp_dev(a, near(j))).wait_recv())

        repeat(0, A, one)

    def w_sent(l, g):
        repeat(1, A, lambda k: wz(l, g, k, a, dp_dev(far(k), b)).wait_send())

        def one(k):
            repeat(1, B, lambda j: wx(l, g, k, j, b, dp_dev(a, near(j))).wait_send())

        repeat(0, A, one)

    def ag_copy(buf, kind):
        row = blk(t) if kind < 2 else blk(flip(2))
        return remote(buf.at[row], buf.at[row], ag_s.at[kind], ag_r.at[kind], ypeer if kind == 0 else sib)

    def ag_start(buf):
        ag_copy(buf, 0).start()
        ag_copy(buf, 1).start()

    def ag_wait(buf, i):
        @pl.when(i == 1)
        def _():
            ref = buf.at[blk(flip(1))]
            remote(ref, ref, ag_s.at[1], ag_r.at[1], sib).wait_recv()

        @pl.when(i == 2)
        def _():
            ref = buf.at[blk(flip(2))]
            remote(ref, ref, ag_s.at[0], ag_r.at[0], ypeer).wait_recv()
            ag_copy(buf, 2).start()

        @pl.when(i == 3)
        def _():
            ref = buf.at[blk(flip(3))]
            remote(ref, ref, ag_s.at[2], ag_r.at[2], sib).wait_recv()
            for kind in range(3):
                ag_copy(buf, kind).wait_send()

    rs_a = remote(SA, RA, rs_s.at[0], rs_r.at[0], sib)
    rs_b = remote(SB, RB, rs_s.at[1], rs_r.at[1], ypeer)
    rs_c = remote(SC, RC, rs_s.at[2], rs_r.at[2], sib)

    def rs_run(part):
        @pl.loop(0, 4)
        def _(step):
            ACC[...] = part(flip(3 - step))

            @pl.when(step == 0)
            def _():
                SA[...] = ACC[...].astype(bf16)
                rs_a.start()

            @pl.when(step == 1)
            def _():
                rs_a.wait_recv()
                SB[...] = (ACC[...] + RA[...].astype(f32)).astype(bf16)
                rs_b.start()

            @pl.when(step == 2)
            def _():
                SC[...] = ACC[...].astype(bf16)
                rs_c.start()

    def rs_wait():
        rs_c.wait_recv()
        rs_b.wait_recv()

    def rs_sum(row):
        return ACC[row, :] + RB[row, :].astype(f32) + RC[row, :].astype(f32)

    def rs_end():
        rs_a.wait_send()
        rs_b.wait_send()
        rs_c.wait_send()

    def by_chunk(body):
        @pl.loop(0, R // CHUNK)
        def _(index):
            body(pl.ds(pl.multiple_of(index * CHUNK, CHUNK), CHUNK), pl.ds(pl.multiple_of(t * R + index * CHUNK, CHUNK), CHUNK))

    def head_mask(h):
        lane = lax.broadcasted_iota(jnp.int32, (R, HC), 1)
        return (lane >= h * HD) & (lane < (h + 1) * HD)

    order = [(l, g) for l in range(2) for g in range(4)]
    w_start(*order[0])
    w_start(*order[1])
    tok_copy.wait()

    def load_tokens(row, full):
        X[0, row, :] = STB[row, :].astype(f32)

    by_chunk(load_tokens)

    def pump(index):
        w_pump(*order[index])
        if index + 2 < len(order):
            w_start(*order[index + 2])

    spills = [
        pltpu.make_async_copy(
            W.at[0, :, pl.ds(first, width)], spill.at[:, pl.ds(first, width)], loc.at[1, 6 + g]
        )
        for g, (first, width) in enumerate(groups)
    ]

    for l in range(2):

        def first_norm(row, full):
            n, _ = norm_parts(X[l, row, :])
            NF[l, full, :] = (n * vec[l, 0:1, :] + vec[l, 1:2, :]).astype(bf16)

        by_chunk(first_norm)
        ag_start(NF.at[l])
        pump(4 * l)
        w_done(l, 0)

        @pl.loop(0, 4)
        def _(i):
            ag_wait(NF.at[l], i)
            row = blk(flip(i))
            out = dot_nn(NF[l, row, :], W[l, :, 0 : 3 * HC])
            QKV[l, row, 0:HC] = (out[:, 0:HC] + vec[l, 7:8, 0:HC]).astype(bf16)
            QKV[l, row, HC : 2 * HC] = out[:, HC : 2 * HC].astype(bf16)
            QKV[l, row, 2 * HC : 3 * HC] = (out[:, 2 * HC : 3 * HC] + vec[l, 7:8, HC : 2 * HC]).astype(bf16)

        VT[...] = QKV[l, :, 2 * HC : 3 * HC].T
        pump(4 * l + 1)
        w_done(l, 1)

        def attend(i):
            row = blk(i)
            queries = QKV[l, row, 0:HC]
            keys = QKV[l, :, HC : 2 * HC]
            outs = []
            for h in range(heads):
                masked = jnp.where(head_mask(h), queries, jnp.zeros_like(queries))
                scores = dot_nt(keys, masked) * (score_scale * LOG2E)
                top = jnp.max(scores, axis=0, keepdims=True)
                exps = jnp.exp2(scores - top)
                total = jnp.sum(exps, axis=0, keepdims=True)
                LSE[l, h : h + 1, row] = top + jnp.log(total) * LOG2E
                outs.append(dot_nn(VT[h * HD : (h + 1) * HD, :], exps.astype(bf16)) * (1.0 / total))
            AT[l, row, :] = jnp.concatenate(outs, axis=0).T.astype(bf16)
            return dot_nt(AT[l, row, :], W[l, :, 3 * HC : 4 * HC])

        rs_run(attend)
        rs_wait()

        def second_norm(row, full):
            middle = X[l, row, :] + rs_sum(row) + vec[l, 2:3, :]
            MID[l, row, :] = middle
            n, _ = norm_parts(middle)
            NF2[l, full, :] = (n * vec[l, 3:4, :] + vec[l, 4:5, :]).astype(bf16)

        by_chunk(second_norm)
        rs_end()
        ag_start(NF2.at[l])
        pump(4 * l + 2)
        w_done(l, 2)

        @pl.loop(0, 4)
        def _(i):
            ag_wait(NF2.at[l], i)
            row = blk(flip(i))
            pre = dot_nn(NF2[l, row, :], W[l, :, 4 * HC : 4 * HC + FC]) + vec[l, 6:7, :]
            cumul = 0.5 * (1.0 + lax.erf(pre * ROOT_HALF))
            ACT[l, row, :] = (pre * cumul).astype(bf16)
            GP[l, row, :] = (cumul + pre * (jnp.exp(-0.5 * pre * pre) * PHI_ZERO)).astype(bf16)

        pump(4 * l + 3)
        w_done(l, 3)
        rs_run(lambda i: dot_nt(ACT[l, blk(i), :], W[l, :, 4 * HC + FC : 4 * HC + 2 * FC]))
        if l == 0:
            for g in range(4):
                w_sent(0, g)
            for copy in spills:
                copy.start()
        rs_wait()

        def layer_out(row, full):
            out = MID[l, row, :] + rs_sum(row) + vec[l, 5:6, :]
            if l == 0:
                X[1, row, :] = out
            else:
                STB[row, :] = out.astype(bf16)

        by_chunk(layer_out)
        rs_end()

    mixed_copy = pltpu.make_async_copy(STB, mixed.at[0], loc.at[0, 6])
    mixed_copy.start()
    for g in range(4):
        w_sent(1, g)
    for copy in spills:
        copy.wait()
    mixed_copy.wait()
    cot_copy = pltpu.make_async_copy(cot.at[0], STB, loc.at[0, 7])
    cot_copy.start()
    cot_copy.wait()
    live = counts[0].astype(f32)

    def load_cot(row, full):
        GC[row, :] = STB[row, :].astype(f32) * live

    by_chunk(load_cot)
    vg[...] = jnp.zeros_like(vg)

    def gsrc(l, g):
        first, width = groups[g]
        if l == 1:
            return W, 0, first, width
        if g == 3:
            return ACT, 1, 0, width
        if g == 2:
            return GP, 1, 0, width
        return NF2, 1, (0 if g == 0 else 3 * HC), width

    def gref(l, g, aa, bb):
        buf, slot, first, width = gsrc(l, g)
        return buf.at[slot, shard(aa, bb), pl.ds(first, width)]

    def gb(l, g, j, aa):
        first, width = groups[g]
        return remote(
            gref(l, g, aa, near(j)), BR.at[j - 1, aa, :, pl.ds(first, width)], gb_s.at[l, g, j, aa], gb_r.at[l, g, j, aa],
            dp_dev(a, near(j)),
        )

    def ga(l, g, k):
        first, width = groups[g]
        return remote(
            gref(l, g, far(k), b), AR.at[k - 1, :, pl.ds(first, width)], ga_s.at[l, g, k], ga_r.at[l, g, k], dp_dev(far(k), b)
        )

    def g_start(l, g):
        if l == 0:
            pl.semaphore_wait(cred_b.at[g], B - 1)

        def one(k):
            repeat(1, B, lambda j: gb(l, g, j, far(k)).start())

        repeat(1, A + 1, one)

    def g_piece(l, g, aa):
        first, width = groups[g]
        repeat(1, B, lambda j: gb(l, g, j, aa).wait_recv())
        total = gref(l, g, aa, b)[...].astype(f32)
        for j in range(1, B):
            total = total + BR[j - 1, aa, :, first : first + width].astype(f32)
        return total

    def g_pump(l, g):
        first, width = groups[g]
        if l == 0:
            pl.semaphore_wait(cred_a.at[g], A - 1)

        def one(k):
            piece = gref(l, g, far(k), b)
            piece[...] = g_piece(l, g, far(k)).astype(bf16)
            ga(l, g, k).start()

        repeat(1, A, one)
        OST[l, :, first : first + width] = g_piece(l, g, a)
        if l == 1:
            repeat(
                1, B,
                lambda j: pl.semaphore_signal(cred_b.at[g], inc=1, device_id=dp_dev(a, near(j)), device_id_type=MESH),
            )

    def g_out(l, g):
        parts = {0: ((gq, 0, HC), (gk, HC, HC), (gv, 2 * HC, HC)), 1: ((go, 0, HC),), 2: ((gu, 0, FC),), 3: ((gd, 0, FC),)}[g]
        first = groups[g][0]
        return [
            pltpu.make_async_copy(
                OST.at[l, :, pl.ds(first + at, width)], dst.at[l], loc.at[l, 2 * g + place if g == 0 else g + 2]
            )
            for place, (dst, at, width) in enumerate(parts)
        ]

    def g_final(l, g):
        first, width = groups[g]

        def one(k):
            ga(l, g, k).wait_recv()
            OST[l, :, first : first + width] += AR[k - 1, :, first : first + width].astype(f32)

        repeat(1, A, one)
        if l == 1:
            repeat(
                1, A,
                lambda k: pl.semaphore_signal(cred_a.at[g], inc=1, device_id=dp_dev(far(k), b), device_id_type=MESH),
            )
        for copy in g_out(l, g):
            copy.start()

    def g_sent(l, g):
        repeat(1, A, lambda k: ga(l, g, k).wait_send())

        def one(k):
            repeat(1, B, lambda j: gb(l, g, j, far(k)).wait_send())

        repeat(1, A + 1, one)
        for copy in g_out(l, g):
            copy.wait()

    def weight_grad(l, g, left, right):
        buf, slot, first, width = gsrc(l, g)

        @pl.loop(0, D // R)
        def _(i):
            buf[slot, blk(i), first : first + width] = dot_tn(left[:, blk(i)], right[...]).astype(bf16)

        g_start(l, g)

    def reload(g):
        first, width = groups[g]
        return pltpu.make_async_copy(spill.at[:, pl.ds(first, width)], W.at[1, :, pl.ds(first, width)], loc.at[1, 6 + g])

    for l in (1, 0):

        def low_grad(row, full):
            low = GC[row, :].astype(bf16)
            GF[full, :] = low
            vg[l, 5:6, :] += jnp.sum(low.astype(f32), axis=0, keepdims=True)

        by_chunk(low_grad)
        ag_start(GF)
        if l == 0:
            reload(3).wait()
            reload(2).wait()
            g_pump(1, 1)

        @pl.loop(0, 4)
        def _(i):
            ag_wait(GF, i)
            row = blk(flip(i))
            act_grad = dot_nn(GF[row, :], W[1, :, 4 * HC + FC : 4 * HC + 2 * FC])
            pre_grad = (act_grad * GP[l, row, :].astype(f32)).astype(bf16)
            GP[l, row, :] = pre_grad
            vg[l, 6:7, :] += jnp.sum(pre_grad.astype(f32), axis=0, keepdims=True)

        rs_run(lambda i: dot_nt(GP[l, blk(i), :], W[1, :, 4 * HC : 4 * HC + FC]))
        if l == 1:
            reload(2).start()
            reload(3).start()
        if l == 0:
            g_pump(1, 0)
        weight_grad(l, 3, GF, ACT.at[l])
        weight_grad(l, 2, NF2.at[l], GP.at[l])
        rs_wait()

        def second_back(row, full):
            dy = rs_sum(row)
            n, scale = norm_parts(MID[l, row, :])
            vg[l, 3:4, :] += jnp.sum(dy * n, axis=0, keepdims=True)
            vg[l, 4:5, :] += jnp.sum(dy, axis=0, keepdims=True)
            dn = dy * vec[l, 3:4, :]
            part = scale * (
                dn - jnp.mean(dn, axis=-1, keepdims=True) - n * jnp.mean(dn * n, axis=-1, keepdims=True)
            )
            grad = GC[row, :] + part
            GC[row, :] = grad
            low = grad.astype(bf16)
            MF[full, :] = low
            vg[l, 2:3, :] += jnp.sum(low.astype(f32), axis=0, keepdims=True)

        by_chunk(second_back)
        rs_end()
        ag_start(MF)
        if l == 0:
            reload(1).wait()
            reload(0).wait()

        @pl.loop(0, 4)
        def _(i):
            ag_wait(MF, i)
            row = blk(flip(i))
            DO[row, :] = dot_nn(MF[row, :], W[1, :, 3 * HC : 4 * HC]).astype(bf16)

        weight_grad(l, 1, MF, AT.at[l])
        if l == 0:
            g_final(1, 1)
            g_final(1, 0)
        g_pump(l, 3)
        if l == 1:
            reload(1).start()
        KT[...] = QKV[l, :, HC : 2 * HC].T
        DKA[...] = jnp.zeros_like(DKA)
        DVA[...] = jnp.zeros_like(DVA)

        @pl.loop(0, 4)
        def _(i):
            row = blk(i)
            queries = QKV[l, row, 0:HC]
            keys = QKV[l, :, HC : 2 * HC]
            values = QKV[l, :, 2 * HC : 3 * HC]
            out_grads = DO[row, :]
            parts = []
            for h in range(heads):
                mask = head_mask(h)
                q_one = jnp.where(mask, queries, jnp.zeros_like(queries))
                do_one = jnp.where(mask, out_grads, jnp.zeros_like(out_grads))
                probs = jnp.exp2(dot_nt(keys, q_one) * (score_scale * LOG2E) - LSE[l, h : h + 1, row])
                prob_grad = dot_nt(values, do_one)
                DVA[...] += dot_nn(probs.astype(bf16), do_one)
                row_dot = jnp.sum(probs * prob_grad, axis=0, keepdims=True)
                score_grad = (probs * (prob_grad - row_dot)).astype(bf16)
                DKA[...] += dot_nn(score_grad, q_one)
                parts.append(dot_nn(KT[h * HD : (h + 1) * HD, :], score_grad))
            DQKV[row, 0:HC] = (jnp.concatenate(parts, axis=0).T * score_scale).astype(bf16)

        g_pump(l, 2)
        DQKV[:, HC : 2 * HC] = (DKA[...] * score_scale).astype(bf16)
        DQKV[:, 2 * HC : 3 * HC] = DVA[...].astype(bf16)
        rs_run(lambda i: dot_nt(DQKV[blk(i), :], W[1, :, 0 : 3 * HC]))
        if l == 1:
            reload(0).start()
        weight_grad(l, 0, NF.at[l], DQKV)
        vg[l, 7:8, 0:HC] = jnp.sum(DQKV[:, 0:HC].astype(f32), axis=0, keepdims=True)
        vg[l, 7:8, HC : 2 * HC] = jnp.sum(DQKV[:, 2 * HC : 3 * HC].astype(f32), axis=0, keepdims=True)
        g_final(l, 3)
        rs_wait()

        def first_back(row, full):
            dy = rs_sum(row)
            n, scale = norm_parts(X[l, row, :])
            vg[l, 0:1, :] += jnp.sum(dy * n, axis=0, keepdims=True)
            vg[l, 1:2, :] += jnp.sum(dy, axis=0, keepdims=True)
            dn = dy * vec[l, 0:1, :]
            part = scale * (
                dn - jnp.mean(dn, axis=-1, keepdims=True) - n * jnp.mean(dn * n, axis=-1, keepdims=True)
            )
            GC[row, :] = GC[row, :] + part

        by_chunk(first_back)
        rs_end()
        g_final(l, 2)

    grad_copy = pltpu.make_async_copy(GC, tgrad.at[0], loc.at[0, 7])
    grad_copy.start()
    g_pump(0, 1)
    g_pump(0, 0)
    g_final(0, 1)
    g_final(0, 0)
    grad_copy.wait()
    for l in range(2):
        for g in range(4):
            g_sent(l, g)


def shards(
    mesh_dp,
    tokens, clip_counts, cotangent, norm1_gain, norm1_shift, w_query, query_bias, w_key, w_value, value_bias, w_out,
    out_bias, norm2_gain, norm2_shift, w_up, up_bias, w_down, down_bias,
):
    t = lax.axis_index("tensor")
    dp = lax.axis_index("dp")
    layers, S, HC = w_query.shape
    FC = w_up.shape[2]
    _, R, D = tokens.shape
    B = 1
    while 4 * B * B <= mesh_dp:
        B *= 2
    A = mesh_dp // B
    packed = jnp.concatenate(
        [
            jnp.stack(
                [norm1_gain, norm1_shift, out_bias, norm2_gain, norm2_shift, down_bias, query_bias, value_bias], axis=1
            ),
            up_bias.reshape(layers, -1, S),
        ],
        axis=1,
    )
    gathered = lax.all_gather(packed, "dp", axis=0)
    wide = gathered[:, :, :8].transpose(1, 2, 0, 3).reshape(layers, 8, D).astype(f32)
    up_full = gathered[:, :, 8:].transpose(1, 0, 2, 3).reshape(layers, 1, -1).astype(f32)
    up_own = lax.dynamic_slice_in_dim(up_full, t * FC, FC, 2)
    heads_own = lax.dynamic_slice_in_dim(wide[:, 6:8], t * HC, HC, 2).reshape(layers, 1, 2 * HC)
    vec = jnp.concatenate([wide[:, :6], up_own, jnp.pad(heads_own, ((0, 0), (0, 0), (0, D - 2 * HC)))], axis=1)

    LEN = 4 * R
    COLS = 4 * HC + 2 * FC
    dims = (A, B, S, R, D, HC, FC)
    vm = pltpu.VMEM
    dma = pltpu.SemaphoreType.DMA
    any_spec = pl.BlockSpec(memory_space=pl.ANY)
    vmem_spec = pl.BlockSpec(memory_space=pltpu.VMEM)
    grad_small = jax.ShapeDtypeStruct((layers, S, HC), f32)
    grad_large = jax.ShapeDtypeStruct((layers, S, FC), f32)
    outs = pl.pallas_call(
        functools.partial(encoder_kernel, dims),
        out_shape=(
            jax.ShapeDtypeStruct((1, R, D), bf16),
            jax.ShapeDtypeStruct((1, R, D), f32),
            grad_small, grad_small, grad_small, grad_small, grad_large, grad_large,
            jax.ShapeDtypeStruct((layers, 8, D), f32),
            jax.ShapeDtypeStruct((D, COLS), bf16),
        ),
        in_specs=[any_spec, any_spec, pl.BlockSpec(memory_space=pltpu.SMEM)] + [any_spec] * 6 + [vmem_spec],
        out_specs=tuple([any_spec] * 8 + [vmem_spec, any_spec]),
        scratch_shapes=[
            vm((2, D, COLS), bf16),
            vm((2, LEN, D), bf16),
            vm((2, LEN, 3 * HC), bf16),
            vm((2, LEN, HC), bf16),
            vm((2, 8, LEN), f32),
            vm((2, R, D), f32),
            vm((2, R, D), f32),
            vm((2, LEN, D), bf16),
            vm((2, LEN, FC), bf16),
            vm((2, LEN, FC), bf16),
            vm((LEN, D), bf16),
            vm((LEN, D), bf16),
            vm((LEN, 3 * HC), bf16),
            vm((LEN, HC), bf16),
            vm((R, D), f32),
            vm((max(B - 1, 1), A, S, COLS), bf16),
            vm((max(A - 1, 1), S, COLS), bf16),
            vm((R, D), bf16), vm((R, D), bf16), vm((R, D), bf16),
            vm((R, D), bf16), vm((R, D), bf16), vm((R, D), bf16),
            vm((R, D), f32),
            vm((2, S, COLS), f32),
            vm((HC, LEN), bf16), vm((HC, LEN), bf16),
            vm((LEN, HC), f32), vm((LEN, HC), f32),
            vm((R, D), bf16),
            dma((2, 10)),
            dma((3,)), dma((3,)), dma((3,)), dma((3,)),
            dma((2, 4, A)), dma((2, 4, A)), dma((2, 4, A, B)), dma((2, 4, A, B)),
            dma((2, 4, B, A)), dma((2, 4, B, A)), dma((2, 4, A)), dma((2, 4, A)),
            pltpu.SemaphoreType.REGULAR((4,)), pltpu.SemaphoreType.REGULAR((4,)),
        ],
        compiler_params=pltpu.CompilerParams(
            collective_id=0, has_side_effects=True, vmem_limit_bytes=64 * 2**20 - 2**17
        ),
        name="encoder",
    )(tokens, cotangent, clip_counts, w_query, w_key, w_value, w_out, w_up, w_down, vec)
    mixed, tokens_grad, gq, gk, gv, go, gu, gd, vg, _ = outs

    def place(part, full):
        return lax.dynamic_update_slice_in_dim(jnp.zeros((layers, full), f32), part, t * part.shape[1], 1)

    whole = jnp.concatenate(
        [vg[:, :6].reshape(layers, -1), place(vg[:, 7, :HC], D), place(vg[:, 7, HC : 2 * HC], D), place(vg[:, 6], 4 * FC)],
        axis=1,
    )
    whole = lax.psum(whole, ("dp", "tensor"))

    def own(index):
        return lax.dynamic_slice_in_dim(whole[:, index * D : (index + 1) * D], dp * S, S, 1)

    ub = lax.dynamic_slice_in_dim(whole[:, 8 * D :], dp * (4 * FC // mesh_dp), 4 * FC // mesh_dp, 1)
    return (
        mixed, tokens_grad, own(0), own(1), gq, own(6), gk, gv, own(7), go, own(2), own(3), own(4), gu, ub, gd, own(5),
    )


def solution(mesh):
    rows = P("dp", "tensor", None)
    vector = P(None, "dp")
    matrix = P(None, "dp", "tensor")
    return jax.shard_map(
        functools.partial(shards, mesh.shape["dp"]),
        mesh=mesh,
        in_specs=(
            rows, P("dp"), rows, vector, vector, matrix, vector, matrix, matrix, vector, matrix, vector, vector, vector,
            matrix, vector, matrix, vector,
        ),
        out_specs=(
            rows, rows, vector, vector, matrix, vector, matrix, matrix, vector, matrix, vector, vector, vector, matrix,
            vector, matrix, vector,
        ),
        check_vma=False,
    )
```

time: 2360 us -> 648 us (0.27)
  waiting for transfers between devices: 1370 us -> 125 us
  blocking collectives: 602 us -> 32.3 us
  Pallas kernels: 0 us -> 447 us
  matrix products: 209 us -> 0 us
  other arithmetic: 80.1 us -> 1.38 us
  local copies, waits for them, and re-layouts: 63.6 us -> 26 us
    reduce_scatter x14 -> x0, waiting for transfers between devices: 709 us -> none  [the longest x1 151 us: shards(): lax.psum_scatter(stacked[11], 'dp', scatter_dimension=1, tiled=True)]
    all_gather x26 -> x1, blocking collectives: 591 us -> 32.3 us  [shards(): gathered = lax.all_gather(packed, 'dp', axis=0)]
    unnamed x44 -> x1, waiting for transfers between devices: 514 us -> 0.02 us
    pallas_call x0 -> x1, Pallas kernels: none -> 447 us  [shards(): pl.pallas_call(functools.partial(encoder_kernel, dims), out_shape=(jax.Sh...]
    dot_general x64 -> x0, matrix products: 209 us -> none  [the longest x12 67.5 us: plain_dot(): return jnp.dot(left_rows, right_rows, preferred_element_type=jnp.float32)]
    all_gather x12 -> x0, waiting for transfers between devices: 151 us -> none  [the longest x2 81.9 us: shards(): lax.all_gather(w_down[layer_index], 'dp', axis=0, tiled=True)]
    psum x0 -> x1, waiting for transfers between devices: none -> 125 us  [shards(): whole = lax.psum(whole, ('dp', 'tensor'))]
    reduce_sum x30 -> x0, other arithmetic: 41.3 us -> none  [the longest x9 12.4 us: layer_norm(): return centered * lax.rsqrt(variance + norm_eps) * gain_vec + shift_vec]
  transfers between devices with their start and end apart: 35 -> 1, of which waited for: 26 -> 1; matrix products, arithmetic and copies ran while one was open for 5% -> 0% of each run, Pallas kernels for 0% -> 0%
where the time goes in v1:
time: 648 us; the launch traced here: 647 us
  Pallas kernels  447 us (69%)
  waiting for transfers between devices  125 us (19%)
  blocking collectives  32.3 us (5%)
  local copies, waits for them, and re-layouts  26 us (4%)
  between operations  14.9 us (2%)
    pallas_call x1, Pallas kernels, shards(): pl.pallas_call(functools.partial(encoder_kernel, dims), out_shape=(jax.Sh...  447 us
    psum x1, waiting for transfers between devices, shards(): whole = lax.psum(whole, ('dp', 'tensor'))  125 us
    all_gather x1, blocking collectives, shards(): gathered = lax.all_gather(packed, 'dp', axis=0)  32.3 us
    unnamed x14, local copies, waits for them, and re-layouts  13.7 us
  transfers between devices with their start and end apart: 1, of which 1 were waited for; matrix products, arithmetic and copies ran while one was open for 0% of the time, Pallas kernels for 0%

profile of v1, /device:TPU:0, one launch (start us, length us, event | category | flops | bytes accessed | tf_op | source)
XLA Modules:
  0.0 646.6 jit_solution(14310165505309837690)
XLA Ops:
  7.2 0.7 reshape.61
  7.9 0.7 copy.48
  8.6 0.7 copy.49
  9.2 0.7 copy.50
  9.9 0.7 copy.51
  10.6 0.7 copy.52
  11.2 0.7 copy.53
  13.3 32.3 %all-gather = bf16[16,12,128]{2,1,0:T(8,128)(2,1)S(1)} all-gather(bf16[2,12,128]{2,1,0:T(8,128)(2,1)S(1)} %concatenate.9), channel_id=2, replica_groups=mesh['dp'=8,'tensor'=4] {'dp'}, dimensions={0}, use_global_device_ids=true | all-gather | bytes 55296 | tf_op jit(solution)/shard_map/all_gather | solution.py:633
  47.0 446.9 %encoder.1 = (bf16[1,256,1024]{2,1,0:T(8,128)(2,1)}, f32[1,256,1024]{2,1,0:T(8,128)}, f32[2,128,256]{2,1,0:T(8,128)}, f32[2,128,256]{2,1,0:T(8,128)}, f32[2,128,...) custom-call(bf16[1,256,1024]{2,1,0:T(8,128)(2,1)} %tok.1, ...), custom_call_target="tpu_custom_call" | custom-call | tf_op jit(solution)/shard_map/encoder/pallas_call | solution.py:649
  494.0 0.9 fusion.1
  494.8 0.8 slice.58
  495.7 0.8 slice_bitcast_fusion
  496.7 0.7 pad_maximum_fusion
  497.4 125.1 %all-reduce.3.cloned.1.call-done = f32[2,12288]{1,0:T(2,128)} async-done(((f32[2,12288]{1,0:T(2,128)}), f32[2,12288]{1,0:T(2,128)}) %all-reduce.3.cloned.1.call-update) | async-done | bytes 98320 | tf_op jit(solution)/shard_map/psum | solution.py:705
  622.5 0.8 fusion
  625.6 0.8 slice.79
  627.0 1.9 copy.81
  628.8 2.3 copy.82
  631.1 1.7 copy.83
  632.8 1.7 copy.84
  634.5 1.7 copy.85
  636.1 1.7 copy.86
  637.8 1.0 copy.87
  638.8 1.0 copy.88
  (31 shorter events, 5.2 us)
Async XLA Ops:
  7.2 615.3 %all-reduce.3.cloned.1.call-start = ((), (), s32[]{:S(2)}) async-start(), calls=%async_computation | async-start | bytes 196608 | tf_op jit(solution)/shard_map/psum | solution.py:705
  493.9 143.9 %copy-start.1 = (f32[2,128,1024]{2,1,0:T(8,128)S(1)}, f32[2,128,1024]{2,1,0:T(8,128)}, u32[]{:S(2)}) copy-start(f32[2,128,1024]{2,1,0:T(8,128)} %get-tuple-element.83) | copy-start | bytes 3145732
  493.9 144.8 %copy-start = (f32[2,128,1024]{2,1,0:T(8,128)S(1)}, f32[2,128,1024]{2,1,0:T(8,128)}, u32[]{:S(2)}) copy-start(f32[2,128,1024]{2,1,0:T(8,128)} %get-tuple-element.85) | copy-start | bytes 3145732
Sparse Core Ops, SparseCore 0:
  497.5 124.9 all-reduce.2

commit v2 on v1

--- a/solution.py
+++ b/solution.py
@@ -37,9 +37,7 @@
             body(index)
     else:
 
-        @pl.loop(low, high)
-        def _(index):
-            body(index)
+        pl.loop(low, high)(body)
 
 
 def norm_parts(rows):
@@ -50,11 +48,12 @@
 
 def encoder_kernel(
     dims,
-    tok, cot, counts, wq, wk, wv, wo, wu, wd, vec,
-    mixed, tgrad, gq, gk, gv, go, gu, gd, vg, spill,
+    tok, cot, counts, wq, wk, wv, wo, wu, wd, gain_one, shift_one, out_b, gain_two, shift_two, down_b, query_b, value_b, up_b,
+    mixed, tgrad, gq, gk, gv, go, gu, gd, vs_out, spill,
     W, NF, QKV, AT, LSE, X, MID, NF2, ACT, GP, GF, MF, DQKV, DO, GC, BR, AR,
-    SA, SB, SC, RA, RB, RC, ACC, OST, VT, KT, DKA, DVA, STB,
-    loc, ag_s, ag_r, rs_s, rs_r, wz_s, wz_r, wx_s, wx_r, gb_s, gb_r, ga_s, ga_r, cred_b, cred_a,
+    SA, SB, SC, RA, RB, RC, ACC, OST, VT, KT, DKA, DVA, STB, RAW, vec, vg, VGX, VGS, VGZ, VGU, VGT, VS, TOT,
+    loc, ag_s, ag_r, rs_s, rs_r, wz_s, wz_r, wx_s, wx_r, gb_s, gb_r, ga_s, ga_r,
+    vz_s, vz_r, vx_s, vx_r, vgx_s, vgx_r, vgz_s, vgz_r, vgt_s, vgt_r, cred_b, cred_a,
 ):
     A, B, S, R, D, HC, FC = dims
     heads = HC // HD
@@ -71,6 +70,7 @@
 
     sib = (dp, flip(1))
     ypeer = (dp, flip(2))
+    corner = (dp, flip(3))
 
     def dp_dev(aa, bb):
         return (aa * B + bb, t)
@@ -101,6 +101,7 @@
 
     greet(sib)
     greet(ypeer)
+    greet(corner)
     repeat(1, A, lambda k: greet(dp_dev(far(k), b)))
     repeat(1, B, lambda j: greet(dp_dev(a, near(j))))
 
@@ -124,7 +125,13 @@
                 copy.start()
     tok_copy = pltpu.make_async_copy(tok.at[0], STB, loc.at[0, 6])
     tok_copy.start()
-    pl.semaphore_wait(barrier, A + B)
+    vectors = (gain_one, shift_one, out_b, gain_two, shift_two, down_b, query_b, value_b)
+    for l in range(2):
+        for place, vector in enumerate(vectors):
+            RAW[dp, 12 * l + place : 12 * l + place + 1, 0:S] = vector[...].astype(f32)[l : l + 1, :]
+        for q in range(4):
+            RAW[dp, 12 * l + 8 + q : 12 * l + 9 + q, 0:S] = up_b[...].astype(f32)[l : l + 1, q * S : (q + 1) * S]
+    pl.semaphore_wait(barrier, A + B + 1)
 
     def wrow(l, aa, bb, g):
         return W.at[l, shard(aa, bb), pl.ds(groups[g][0], groups[g][1])]
@@ -144,14 +151,13 @@
         for copy in load_weight(l, g):
             copy.wait()
         repeat(1, A, lambda k: wz(l, g, k, a, dp_dev(far(k), b)).start())
-        w_send_x(l, g, 0)
-
-    def w_pump(l, g):
-        def one(k):
-            wz(l, g, k, (a - k + A) % A, dp_dev(far(k), b)).wait_recv()
-            w_send_x(l, g, k)
-
-        repeat(1, A, one)
+
+    def w_pass(l, g, k):
+        wz(l, g, k, (a - k + A) % A, dp_dev(far(k), b)).wait_recv()
+        w_send_x(l, g, k)
+
+    def w_pump(l, g, first=1, last=None):
+        repeat(first, A if last is None else last + 1, lambda k: w_pass(l, g, k))
 
     def w_done(l, g):
         def one(k):
@@ -198,9 +204,11 @@
     rs_b = remote(SB, RB, rs_s.at[1], rs_r.at[1], ypeer)
     rs_c = remote(SC, RC, rs_s.at[2], rs_r.at[2], sib)
 
-    def rs_run(part):
+    def rs_run(part, hooks={}):
         @pl.loop(0, 4)
         def _(step):
+            for place, hook in hooks.items():
+                pl.when(step == place)(hook)
             ACC[...] = part(flip(3 - step))
 
             @pl.when(step == 0)
@@ -240,20 +248,70 @@
         lane = lax.broadcasted_iota(jnp.int32, (R, HC), 1)
         return (lane >= h * HD) & (lane < (h + 1) * HD)
 
-    order = [(l, g) for l in range(2) for g in range(4)]
-    w_start(*order[0])
-    w_start(*order[1])
+    def vz(k, source, device):
+        ref = RAW.at[source * B + b]
+        return remote(ref, ref, vz_s.at[k], vz_r.at[k], device)
+
+    def vx(k, j, minor, device):
+        ref = RAW.at[(a - k + A) % A * B + minor]
+        return remote(ref, ref, vx_s.at[k, j], vx_r.at[k, j], device)
+
+    def v_send_x(k):
+        repeat(1, B, lambda j: vx(k, j, b, dp_dev(a, near(j))).start())
+
+    def v_pass(k):
+        vz(k, (a - k + A) % A, dp_dev(far(k), b)).wait_recv()
+        v_send_x(k)
+
+    def v_done(k):
+        repeat(1, B, lambda j: vx(k, j, (b - j + B) % B, dp_dev(a, near(j))).wait_recv())
+
+    def v_sent(k):
+        repeat(1, B, lambda j: vx(k, j, b, dp_dev(a, near(j))).wait_send())
+
+    repeat(1, A, lambda k: vz(k, a, dp_dev(far(k), b)).start())
+    v_send_x(0)
+
+    w_start(0, 0)
+    w_send_x(0, 0, 0)
     tok_copy.wait()
 
     def load_tokens(row, full):
         X[0, row, :] = STB[row, :].astype(f32)
 
     by_chunk(load_tokens)
-
-    def pump(index):
-        w_pump(*order[index])
-        if index + 2 < len(order):
-            w_start(*order[index + 2])
+    for g in range(1, 4):
+        w_start(0, g)
+        w_send_x(0, g, 0)
+    for g in range(4):
+        w_start(1, g)
+    repeat(1, A, v_pass)
+    repeat(0, A, v_done)
+    repeat(1, A, lambda k: vz(k, a, dp_dev(far(k), b)).wait_send())
+    repeat(0, A, v_sent)
+
+    quarter = A * B // 4
+
+    def lay_out(row, offset, pieces):
+        per_tile = max(1, 128 // S)
+        for start in range(0, len(pieces), per_tile):
+            run = pieces[start : start + per_tile]
+            value = run[0] if len(run) == 1 else jnp.concatenate([piece[:, 0:S] for piece in run], axis=1)
+            at = offset + start * S
+            vec[row[0], row[1] : row[1] + 1, at : at + len(run) * S] = value[:, 0 : len(run) * S]
+
+    for l in range(2):
+        for place in range(6):
+            lay_out((l, place), 0, [RAW[d, 12 * l + place : 12 * l + place + 1, :] for d in range(A * B)])
+        for place in range(2):
+            lay_out(
+                (l, 7), place * HC,
+                [RAW[t * quarter + d, 12 * l + 6 + place : 12 * l + 7 + place, :] for d in range(quarter)],
+            )
+        lay_out(
+            (l, 6), 0,
+            [RAW[t * quarter + d, 12 * l + 8 + q : 12 * l + 9 + q, :] for d in range(quarter) for q in range(4)],
+        )
 
     spills = [
         pltpu.make_async_copy(
@@ -270,7 +328,12 @@
 
         by_chunk(first_norm)
         ag_start(NF.at[l])
-        pump(4 * l)
+        if l == 0:
+            w_pump(0, 0)
+        w_pump(l, 1)
+        if l == 0:
+            w_send_x(1, 0, 0)
+            w_send_x(1, 1, 0)
         w_done(l, 0)
 
         @pl.loop(0, 4)
@@ -283,7 +346,6 @@
             QKV[l, row, 2 * HC : 3 * HC] = (out[:, 2 * HC : 3 * HC] + vec[l, 7:8, HC : 2 * HC]).astype(bf16)
 
         VT[...] = QKV[l, :, 2 * HC : 3 * HC].T
-        pump(4 * l + 1)
         w_done(l, 1)
 
         def attend(i):
@@ -302,7 +364,8 @@
             AT[l, row, :] = jnp.concatenate(outs, axis=0).T.astype(bf16)
             return dot_nt(AT[l, row, :], W[l, :, 3 * HC : 4 * HC])
 
-        rs_run(attend)
+        rs_run(attend, {2: lambda: w_pass(l, 2, 1), 3: lambda: w_pump(l, 2, 2, A - 2)})
+        w_pass(l, 2, A - 1)
         rs_wait()
 
         def second_norm(row, full):
@@ -314,11 +377,15 @@
         by_chunk(second_norm)
         rs_end()
         ag_start(NF2.at[l])
-        pump(4 * l + 2)
         w_done(l, 2)
+        w_pass(l, 3, 1)
 
         @pl.loop(0, 4)
         def _(i):
+            @pl.when(i == 2)
+            def _():
+                w_pump(l, 3, 2, A - 2)
+
             ag_wait(NF2.at[l], i)
             row = blk(flip(i))
             pre = dot_nn(NF2[l, row, :], W[l, :, 4 * HC : 4 * HC + FC]) + vec[l, 6:7, :]
@@ -326,14 +393,15 @@
             ACT[l, row, :] = (pre * cumul).astype(bf16)
             GP[l, row, :] = (cumul + pre * (jnp.exp(-0.5 * pre * pre) * PHI_ZERO)).astype(bf16)
 
-        pump(4 * l + 3)
+        w_pass(l, 3, A - 1)
+        if l == 0:
+            w_send_x(1, 2, 0)
+            w_send_x(1, 3, 0)
         w_done(l, 3)
         rs_run(lambda i: dot_nt(ACT[l, blk(i), :], W[l, :, 4 * HC + FC : 4 * HC + 2 * FC]))
         if l == 0:
-            for g in range(4):
-                w_sent(0, g)
-            for copy in spills:
-                copy.start()
+            w_pass(1, 0, 1)
+            w_pump(1, 0, 2, A - 2)
         rs_wait()
 
         def layer_out(row, full):
@@ -345,6 +413,12 @@
 
         by_chunk(layer_out)
         rs_end()
+        if l == 0:
+            w_pass(1, 0, A - 1)
+            for g in range(4):
+                w_sent(0, g)
+            for copy in spills:
+                copy.start()
 
     mixed_copy = pltpu.make_async_copy(STB, mixed.at[0], loc.at[0, 6])
     mixed_copy.start()
@@ -408,17 +482,18 @@
             total = total + BR[j - 1, aa, :, first : first + width].astype(f32)
         return total
 
-    def g_pump(l, g):
+    def g_pass(l, g, k):
+        piece = gref(l, g, far(k), b)
+        piece[...] = g_piece(l, g, far(k)).astype(bf16)
+        ga(l, g, k).start()
+
+    def g_pump(l, g, first=1, last=None):
+        if l == 0 and first == 1:
+            pl.semaphore_wait(cred_a.at[g], A - 1)
+        repeat(first, A if last is None else last + 1, lambda k: g_pass(l, g, k))
+
+    def g_own(l, g):
         first, width = groups[g]
-        if l == 0:
-            pl.semaphore_wait(cred_a.at[g], A - 1)
-
-        def one(k):
-            piece = gref(l, g, far(k), b)
-            piece[...] = g_piece(l, g, far(k)).astype(bf16)
-            ga(l, g, k).start()
-
-        repeat(1, A, one)
         OST[l, :, first : first + width] = g_piece(l, g, a)
         if l == 1:
             repeat(
@@ -475,6 +550,58 @@
         first, width = groups[g]
         return pltpu.make_async_copy(spill.at[:, pl.ds(first, width)], W.at[1, :, pl.ds(first, width)], loc.at[1, 6 + g])
 
+    def vgx(l, j):
+        return remote(vg.at[l], VGX.at[l, j - 1], vgx_s.at[l, j], vgx_r.at[l, j], dp_dev(a, near(j)))
+
+    def vgz(l, k):
+        return remote(VGS.at[l], VGZ.at[l, k - 1], vgz_s.at[l, k], vgz_r.at[l, k], dp_dev(far(k), b))
+
+    def vgt(l, i):
+        return remote(VGU.at[l], VGT.at[l, i - 1], vgt_s.at[l, i], vgt_r.at[l, i], (dp, flip(i)))
+
+    def vg_near(l):
+        repeat(1, B, lambda j: vgx(l, j).start())
+
+    def vg_far(l):
+        repeat(1, B, lambda j: vgx(l, j).wait_recv())
+        VGS[l] = vg[l]
+        for j in range(1, B):
+            VGS[l] += VGX[l, j - 1]
+        repeat(1, A, lambda k: vgz(l, k).start())
+
+    def vg_tensor(l):
+        repeat(1, A, lambda k: vgz(l, k).wait_recv())
+        VGU[l] = VGS[l]
+        for k in range(1, A):
+            VGU[l] += VGZ[l, k - 1]
+        repeat(1, 4, lambda i: vgt(l, i).start())
+
+    def own_lanes(ref, start):
+        if S % 128 == 0:
+            return ref[:, pl.ds(pl.multiple_of(start, 128), S)]
+        tile = ref[:, pl.ds(pl.multiple_of(start // 128 * 128, 128), 128)]
+        return pltpu.roll(tile, (128 - start % 128) % 128, 1)[:, 0:S]
+
+    def vg_end(l):
+        repeat(1, 4, lambda i: vgt(l, i).wait_recv())
+        owner = dp // quarter
+        total = VGU[l]
+        picked = jnp.where(flip(0) == owner, VGU[l], 0.0)
+        for i in range(1, 4):
+            total = total + VGT[l, i - 1]
+            picked = picked + jnp.where(flip(i) == owner, VGT[l, i - 1], 0.0)
+        TOT[0:8, :] = total
+        TOT[8:16, :] = picked
+        inside = dp % quarter
+        VS[l, 0:6, 0:S] = own_lanes(TOT.at[0:8], dp * S)[0:6, :]
+        VS[l, 6:7, 0:S] = own_lanes(TOT.at[8:16], inside * S)[7:8, :]
+        VS[l, 7:8, 0:S] = own_lanes(TOT.at[8:16], HC + inside * S)[7:8, :]
+        for q in range(4):
+            VS[l, 8 + q : 9 + q, 0:S] = own_lanes(TOT.at[8:16], inside * 4 * S + q * S)[6:7, :]
+        repeat(1, B, lambda j: vgx(l, j).wait_send())
+        repeat(1, A, lambda k: vgz(l, k).wait_send())
+        repeat(1, 4, lambda i: vgt(l, i).wait_send())
+
     for l in (1, 0):
 
         def low_grad(row, full):
@@ -487,10 +614,17 @@
         if l == 0:
             reload(3).wait()
             reload(2).wait()
-            g_pump(1, 1)
+            g_own(1, 1)
+            g_pass(1, 0, 1)
 
         @pl.loop(0, 4)
         def _(i):
+            if l == 0:
+
+                @pl.when(i == 2)
+                def _():
+                    g_pump(1, 0, 2, A - 2)
+
             ag_wait(GF, i)
             row = blk(flip(i))
             act_grad = dot_nn(GF[row, :], W[1, :, 4 * HC + FC : 4 * HC + 2 * FC])
@@ -498,14 +632,19 @@
             GP[l, row, :] = pre_grad
             vg[l, 6:7, :] += jnp.sum(pre_grad.astype(f32), axis=0, keepdims=True)
 
+        if l == 0:
+            g_pass(1, 0, A - 1)
+            vg_far(1)
         rs_run(lambda i: dot_nt(GP[l, blk(i), :], W[1, :, 4 * HC : 4 * HC + FC]))
         if l == 1:
             reload(2).start()
             reload(3).start()
         if l == 0:
-            g_pump(1, 0)
+            g_own(1, 0)
         weight_grad(l, 3, GF, ACT.at[l])
         weight_grad(l, 2, NF2.at[l], GP.at[l])
+        if l == 0:
+            vg_tensor(1)
         rs_wait()
 
         def second_back(row, full):
@@ -527,8 +666,11 @@
         rs_end()
         ag_start(MF)
         if l == 0:
+            g_final(1, 2)
+            g_final(1, 1)
             reload(1).wait()
             reload(0).wait()
+        g_pump(l, 3, 1, A - 2)
 
         @pl.loop(0, 4)
         def _(i):
@@ -538,9 +680,8 @@
 
         weight_grad(l, 1, MF, AT.at[l])
         if l == 0:
-            g_final(1, 1)
             g_final(1, 0)
-        g_pump(l, 3)
+        g_pass(l, 3, A - 1)
         if l == 1:
             reload(1).start()
         KT[...] = QKV[l, :, HC : 2 * HC].T
@@ -549,6 +690,14 @@
 
         @pl.loop(0, 4)
         def _(i):
+            @pl.when(i == 1)
+            def _():
+                g_own(l, 3)
+
+            @pl.when(i == 3)
+            def _():
+                g_pump(l, 2, 1, 1)
+
             row = blk(i)
             queries = QKV[l, row, 0:HC]
             keys = QKV[l, :, HC : 2 * HC]
@@ -568,7 +717,7 @@
                 parts.append(dot_nn(KT[h * HD : (h + 1) * HD, :], score_grad))
             DQKV[row, 0:HC] = (jnp.concatenate(parts, axis=0).T * score_scale).astype(bf16)
 
-        g_pump(l, 2)
+        g_pump(l, 2, 2, A - 2)
         DQKV[:, HC : 2 * HC] = (DKA[...] * score_scale).astype(bf16)
         DQKV[:, 2 * HC : 3 * HC] = DVA[...].astype(bf16)
         rs_run(lambda i: dot_nt(DQKV[blk(i), :], W[1, :, 0 : 3 * HC]))
@@ -577,7 +726,11 @@
         weight_grad(l, 0, NF.at[l], DQKV)
         vg[l, 7:8, 0:HC] = jnp.sum(DQKV[:, 0:HC].astype(f32), axis=0, keepdims=True)
         vg[l, 7:8, HC : 2 * HC] = jnp.sum(DQKV[:, 2 * HC : 3 * HC].astype(f32), axis=0, keepdims=True)
+        g_pass(l, 2, A - 1)
+        g_own(l, 2)
         g_final(l, 3)
+        if l == 0:
+            vg_end(1)
         rs_wait()
 
         def first_back(row, full):
@@ -593,18 +746,51 @@
 
         by_chunk(first_back)
         rs_end()
-        g_final(l, 2)
+        vg_near(l)
+        if l == 1:
+            g_pump(1, 1)
 
     grad_copy = pltpu.make_async_copy(GC, tgrad.at[0], loc.at[0, 7])
     grad_copy.start()
     g_pump(0, 1)
+    vg_far(0)
+    g_own(0, 1)
     g_pump(0, 0)
+    vg_tensor(0)
+    g_final(0, 2)
     g_final(0, 1)
+    g_own(0, 0)
+    vg_end(0)
+    vs_copy = pltpu.make_async_copy(VS, vs_out, loc.at[0, 6])
+    vs_copy.start()
     g_final(0, 0)
     grad_copy.wait()
+    vs_copy.wait()
     for l in range(2):
         for g in range(4):
             g_sent(l, g)
+
+
+def finish_kernel(S, *refs):
+    sources, small, targets, smalls, stages, sems = refs[:8], refs[8], refs[9:17], refs[17:26], refs[26:34], refs[34]
+    arrivals = [
+        pltpu.make_async_copy(source, stage, sems.at[0, at]) for at, (source, stage) in enumerate(zip(sources, stages))
+    ]
+    copies = [
+        pltpu.make_async_copy(stage, target, sems.at[1, at]) for at, (stage, target) in enumerate(zip(stages, targets))
+    ]
+    for arrival in arrivals:
+        arrival.start()
+    for arrival, copy in zip(arrivals, copies):
+        arrival.wait()
+        copy.start()
+    for l in range(2):
+        for place in range(8):
+            smalls[place][l : l + 1, :] = small[l, place : place + 1, 0:S]
+        for q in range(4):
+            smalls[8][l : l + 1, q * S : (q + 1) * S] = small[l, 8 + q : 9 + q, 0:S]
+    for copy in copies:
+        copy.wait()
 
 
 def shards(
@@ -612,8 +798,6 @@
     tokens, clip_counts, cotangent, norm1_gain, norm1_shift, w_query, query_bias, w_key, w_value, value_bias, w_out,
     out_bias, norm2_gain, norm2_shift, w_up, up_bias, w_down, down_bias,
 ):
-    t = lax.axis_index("tensor")
-    dp = lax.axis_index("dp")
     layers, S, HC = w_query.shape
     FC = w_up.shape[2]
     _, R, D = tokens.shape
@@ -621,22 +805,6 @@
     while 4 * B * B <= mesh_dp:
         B *= 2
     A = mesh_dp // B
-    packed = jnp.concatenate(
-        [
-            jnp.stack(
-                [norm1_gain, norm1_shift, out_bias, norm2_gain, norm2_shift, down_bias, query_bias, value_bias], axis=1
-            ),
-            up_bias.reshape(layers, -1, S),
-        ],
-        axis=1,
-    )
-    gathered = lax.all_gather(packed, "dp", axis=0)
-    wide = gathered[:, :, :8].transpose(1, 2, 0, 3).reshape(layers, 8, D).astype(f32)
-    up_full = gathered[:, :, 8:].transpose(1, 0, 2, 3).reshape(layers, 1, -1).astype(f32)
-    up_own = lax.dynamic_slice_in_dim(up_full, t * FC, FC, 2)
-    heads_own = lax.dynamic_slice_in_dim(wide[:, 6:8], t * HC, HC, 2).reshape(layers, 1, 2 * HC)
-    vec = jnp.concatenate([wide[:, :6], up_own, jnp.pad(heads_own, ((0, 0), (0, 0), (0, D - 2 * HC)))], axis=1)
-
     LEN = 4 * R
     COLS = 4 * HC + 2 * FC
     dims = (A, B, S, R, D, HC, FC)
@@ -652,11 +820,11 @@
             jax.ShapeDtypeStruct((1, R, D), bf16),
             jax.ShapeDtypeStruct((1, R, D), f32),
             grad_small, grad_small, grad_small, grad_small, grad_large, grad_large,
-            jax.ShapeDtypeStruct((layers, 8, D), f32),
+            jax.ShapeDtypeStruct((layers, 16, 128), f32),
             jax.ShapeDtypeStruct((D, COLS), bf16),
         ),
-        in_specs=[any_spec, any_spec, pl.BlockSpec(memory_space=pltpu.SMEM)] + [any_spec] * 6 + [vmem_spec],
-        out_specs=tuple([any_spec] * 8 + [vmem_spec, any_spec]),
+        in_specs=[any_spec, any_spec, pl.BlockSpec(memory_space=pltpu.SMEM)] + [any_spec] * 6 + [vmem_spec] * 9,
+        out_specs=tuple([any_spec] * 10),
         scratch_shapes=[
             vm((2, D, COLS), bf16),
             vm((2, LEN, D), bf16),
@@ -682,34 +850,45 @@
             vm((HC, LEN), bf16), vm((HC, LEN), bf16),
             vm((LEN, HC), f32), vm((LEN, HC), f32),
             vm((R, D), bf16),
+            vm((A * B, 24, 128), f32),
+            vm((2, 8, D), f32), vm((2, 8, D), f32),
+            vm((2, max(B - 1, 1), 8, D), f32),
+            vm((2, 8, D), f32),
+            vm((2, max(A - 1, 1), 8, D), f32),
+            vm((2, 8, D), f32),
+            vm((2, 3, 8, D), f32),
+            vm((2, 16, 128), f32),
+            vm((16, D), f32),
             dma((2, 10)),
             dma((3,)), dma((3,)), dma((3,)), dma((3,)),
             dma((2, 4, A)), dma((2, 4, A)), dma((2, 4, A, B)), dma((2, 4, A, B)),
             dma((2, 4, B, A)), dma((2, 4, B, A)), dma((2, 4, A)), dma((2, 4, A)),
+            dma((A,)), dma((A,)), dma((A, B)), dma((A, B)),
+            dma((2, B)), dma((2, B)), dma((2, A)), dma((2, A)), dma((2, 4)), dma((2, 4)),
             pltpu.SemaphoreType.REGULAR((4,)), pltpu.SemaphoreType.REGULAR((4,)),
         ],
         compiler_params=pltpu.CompilerParams(
             collective_id=0, has_side_effects=True, vmem_limit_bytes=64 * 2**20 - 2**17
         ),
         name="encoder",
-    )(tokens, cotangent, clip_counts, w_query, w_key, w_value, w_out, w_up, w_down, vec)
-    mixed, tokens_grad, gq, gk, gv, go, gu, gd, vg, _ = outs
-
-    def place(part, full):
-        return lax.dynamic_update_slice_in_dim(jnp.zeros((layers, full), f32), part, t * part.shape[1], 1)
-
-    whole = jnp.concatenate(
-        [vg[:, :6].reshape(layers, -1), place(vg[:, 7, :HC], D), place(vg[:, 7, HC : 2 * HC], D), place(vg[:, 6], 4 * FC)],
-        axis=1,
-    )
-    whole = lax.psum(whole, ("dp", "tensor"))
-
-    def own(index):
-        return lax.dynamic_slice_in_dim(whole[:, index * D : (index + 1) * D], dp * S, S, 1)
-
-    ub = lax.dynamic_slice_in_dim(whole[:, 8 * D :], dp * (4 * FC // mesh_dp), 4 * FC // mesh_dp, 1)
+    )(tokens, cotangent, clip_counts, w_query, w_key, w_value, w_out, w_up, w_down, norm1_gain, norm1_shift,
+      out_bias, norm2_gain, norm2_shift, down_bias, query_bias, value_bias, up_bias)
+
+    small = jax.ShapeDtypeStruct((layers, S), f32)
+    large_types = tuple(jax.ShapeDtypeStruct(member.shape, member.dtype) for member in outs[:8])
+    (mixed, tokens_grad, gq, gk, gv, go, gu, gd, g_gain_one, g_shift_one, g_out, g_gain_two, g_shift_two, g_down, g_query,
+     g_value, g_up) = pl.pallas_call(
+        functools.partial(finish_kernel, S),
+        out_shape=large_types + (small,) * 8 + (jax.ShapeDtypeStruct((layers, 4 * S), f32),),
+        in_specs=[any_spec] * 8 + [vmem_spec],
+        out_specs=tuple([any_spec] * 8 + [vmem_spec] * 9),
+        scratch_shapes=[vm(member.shape, member.dtype) for member in outs[:8]] + [dma((2, 8))],
+        compiler_params=pltpu.CompilerParams(vmem_limit_bytes=64 * 2**20 - 2**17),
+        name="finish",
+    )(*outs[:9])
     return (
-        mixed, tokens_grad, own(0), own(1), gq, own(6), gk, gv, own(7), go, own(2), own(3), own(4), gu, ub, gd, own(5),
+        mixed, tokens_grad, g_gain_one, g_shift_one, gq, g_query, gk, gv, g_value, go, g_out, g_gain_two, g_shift_two, gu,
+        g_up, gd, g_down,
     )
 
 

time: 648 us -> 418 us (0.65)
  waiting for transfers between devices: 125 us -> 0 us
  Pallas kernels: 447 us -> 413 us
  blocking collectives: 32.3 us -> 0 us
  local copies, waits for them, and re-layouts: 26 us -> 0 us
  between operations: 14.9 us -> 1.5 us
    psum x1 -> x0, waiting for transfers between devices: 125 us -> none  [shards(): whole = lax.psum(whole, ('dp', 'tensor'))]
    pallas_call x1, Pallas kernels: 447 us -> 408 us  [shards(): pl.pallas_call(functools.partial(encoder_kernel, dims), out_shape=(jax.Sh...]
    all_gather x1 -> x0, blocking collectives: 32.3 us -> none  [shards(): gathered = lax.all_gather(packed, 'dp', axis=0)]
    unnamed x14 -> x0, local copies, waits for them, and re-layouts: 13.7 us -> none
  transfers between devices with their start and end apart: 1 -> 0, of which waited for: 1 -> 0; matrix products, arithmetic and copies ran while one was open for 0% -> 0% of each run, Pallas kernels for 0% -> 0%
where the time goes in v2:
time: 418 us; the launch traced here: 415 us
  Pallas kernels  413 us (99%)
    pallas_call x1, Pallas kernels, shards(): pl.pallas_call(functools.partial(encoder_kernel, dims), out_shape=(jax.Sh...  408 us

profile of v2, /device:TPU:0, one launch (start us, length us, event | category | flops | bytes accessed | tf_op | source)
XLA Modules:
  0.0 415.0 jit_solution(4191631079324308515)
XLA Ops:
  1.3 408.0 %encoder.1 = (bf16[1,256,1024]{2,1,0:T(8,128)(2,1)}, f32[1,256,1024]{2,1,0:T(8,128)}, f32[2,128,256]{2,1,0:T(8,128)}, f32[2,128,256]{2,1,0:T(8,128)}, f32[2,128,...) custom-call(bf16[1,256,1024]{2,1,0:T(8,128)(2,1)} %tok.1, ...), custom_call_target="tpu_custom_call" | custom-call | tf_op jit(solution)/shard_map/encoder/pallas_call | solution.py:817
  409.3 5.5 %finish.1 = (bf16[1,256,1024]{2,1,0:T(8,128)(2,1)}, f32[1,256,1024]{2,1,0:T(8,128)}, f32[2,128,256]{2,1,0:T(8,128)}, f32[2,128,256]{2,1,0:T(8,128)}, f32[2,128,2...) custom-call(bf16[1,256,1024]{2,1,0:T(8,128)(2,1)} %get-tuple-element, ...), custom_call_target="tpu_custom_call" | custom-call | tf_op jit(solution)/shard_map/finish/pallas_call | solution.py:880

commit v3 on v2

v3 whole, which is shorter than its diff:
```python
import functools
import math

import jax
import jax.numpy as jnp
from jax import lax
from jax.experimental import pallas as pl
from jax.experimental.pallas import tpu as pltpu
from jax.sharding import PartitionSpec as P

HD = 64
norm_eps = 1e-06
MESH = pl.DeviceIdType.MESH
bf16 = jnp.bfloat16
f32 = jnp.float32
ROOT_HALF = 1.0 / math.sqrt(2.0)
PHI_ZERO = 1.0 / math.sqrt(2.0 * math.pi)
LOG2E = 1.0 / math.log(2.0)
CHUNK = 64
SCHEDULE = (0, 16, 4, 16, 20, 20, 24, 28, 36, 40, 44, 48, 48, 52, 52, 56, 60, 60, 64, 64, 76, 80, 92, 96, 32, 72)


def dot_nn(left, right):
    return jnp.dot(left, right, preferred_element_type=f32)


def dot_nt(left, right):
    return lax.dot_general(left, right, (((1,), (1,)), ((), ())), preferred_element_type=f32)


def dot_tn(left, right):
    return lax.dot_general(left, right, (((0,), (0,)), ((), ())), preferred_element_type=f32)


def repeat(low, high, body):
    if high - low <= 4:
        for index in range(low, high):
            body(index)
    else:

        pl.loop(low, high)(body)


def norm_parts(rows):
    centered = rows - jnp.mean(rows, axis=-1, keepdims=True)
    scale = lax.rsqrt(jnp.mean(centered * centered, axis=-1, keepdims=True) + norm_eps)
    return centered * scale, scale


def encoder_kernel(
    dims,
    tok, cot, counts, wq, wk, wv, wo, wu, wd, gain_one, shift_one, out_b, gain_two, shift_two, down_b, query_b, value_b, up_b,
    mixed, tgrad, gq, gk, gv, go, gu, gd, vs_out, spill,
    W, NF, QKV, AT, LSE, X, MID, NF2, ACT, GP, GF, MF, DQKV, GC, BR, AR,
    SA, SB, SC, RA, RB, RC, ACC, PBUF, OST, TR, DKA, STB, RAW, vec, vg, VGX, VGS, VGZ, VGU, VGT, VS, TOT,
    loc, ag_s, ag_r, rs_s, rs_r, wz_s, wz_r, wx_s, wx_r, gb_s, gb_r, ga_s, ga_r,
    vz_s, vz_r, vx_s, vx_r, vgx_s, vgx_r, vgz_s, vgz_r, vgt_s, vgt_r, cred_b, cred_a, ack,
):
    A, B, S, R, D, HC, FC = dims
    heads = HC // HD
    score_scale = HD ** (-0.5)
    dp = lax.axis_index("dp")
    t = lax.axis_index("tensor")
    a = dp // B
    b = dp % B
    y = t // 2
    c = t % 2

    def flip(i):
        return 2 * ((y + i // 2) % 2) + (c + i % 2) % 2

    sib = (dp, flip(1))
    ypeer = (dp, flip(2))
    corner = (dp, flip(3))

    def dp_dev(aa, bb):
        return (aa * B + bb, t)

    def far(k):
        return (a + k) % A

    def near(j):
        return (b + j) % B

    fine = A * B <= 16
    spans = {"qkv": (0, 3 * HC), "out": (3 * HC, HC), "up": (4 * HC, FC), "down": (4 * HC + FC, FC)}
    groups, sets = [], {}
    for name, (first, width) in spans.items():
        step = HC if fine else width
        sets[name] = tuple(range(len(groups), len(groups) + width // step))
        groups.extend((at, step) for at in range(first, first + width, step))

    def part(pieces, low, high, parts):
        return pieces[low * len(pieces) // parts : high * len(pieces) // parts]

    half = R // 2
    quarter = A * B // 4

    def own_half(h):
        return pl.ds(pl.multiple_of(h * half, half), half)

    def hrow(i, h):
        return pl.ds(pl.multiple_of(i * R + h * half, half), half)

    def near_pair(h):
        return hrow(flip(1), h), hrow(flip(0), h)

    def far_pair(h):
        return hrow(flip(3), h), hrow(flip(2), h)

    def pair(near, h):
        return hrow(flip(3 - 2 * near), h), hrow(flip(2 - 2 * near), h)

    def both(ref, rows):
        return jnp.concatenate([ref[rows[0], :], ref[rows[1], :]], axis=0)

    def put(ref, rows, value):
        ref[rows[0], :] = value[0:half]
        ref[rows[1], :] = value[half : 2 * half]

    def blk(i):
        return pl.ds(pl.multiple_of(i * R, R), R)

    def shard(aa, bb):
        return pl.ds(pl.multiple_of((aa * B + bb) * S, S), S)

    def remote(src, dst, send, recv, device):
        return pltpu.make_async_remote_copy(
            src_ref=src, dst_ref=dst, send_sem=send, recv_sem=recv, device_id=device, device_id_type=MESH
        )

    barrier = pltpu.get_barrier_semaphore()

    def greet(device):
        pl.semaphore_signal(barrier, inc=1, device_id=device, device_id_type=MESH)

    greet(sib)
    greet(ypeer)
    greet(corner)
    repeat(1, A, lambda k: greet(dp_dev(far(k), b)))
    repeat(1, B, lambda j: greet(dp_dev(a, near(j))))

    weights = (
        (wq, 0, HC), (wk, HC, HC), (wv, 2 * HC, HC), (wo, 3 * HC, HC), (wu, 4 * HC, FC), (wd, 4 * HC + FC, FC),
    )
    loads = {
        (l, at): pltpu.make_async_copy(src.at[l], W.at[l, shard(a, b), pl.ds(first, width)], loc.at[l, at])
        for l in range(2)
        for at, (src, first, width) in enumerate(weights)
    }
    for copy in loads.values():
        copy.start()
    tok_copy = pltpu.make_async_copy(tok.at[0], STB, loc.at[0, 6])
    tok_copy.start()
    cot_copy = pltpu.make_async_copy(cot.at[0], STB, loc.at[0, 7])
    live = counts[0].astype(f32)
    vg[...] = jnp.zeros_like(vg)
    vectors = (gain_one, shift_one, out_b, gain_two, shift_two, down_b, query_b, value_b)
    for l in range(2):
        for place, vector in enumerate(vectors):
            RAW[dp, 12 * l + place : 12 * l + place + 1, 0:S] = vector[...].astype(f32)[l : l + 1, :]
        for q in range(4):
            RAW[dp, 12 * l + 8 + q : 12 * l + 9 + q, 0:S] = up_b[...].astype(f32)[l : l + 1, q * S : (q + 1) * S]
    pl.semaphore_wait(barrier, A + B + 1)

    order = [(l, g) for l in range(2) for g in range(len(groups))]

    def wrow(n, source, minor):
        l, g = order[n]
        return W.at[l, shard(source, minor), pl.ds(groups[g][0], groups[g][1])]

    def wz(n, way, hop, source):
        ref = wrow(n, source, b)
        return remote(ref, ref, wz_s.at[n, way, hop], wz_r.at[n, way, hop], dp_dev(a + 1 - 2 * way, b))

    def wx(n, behind, j, minor):
        ref = wrow(n, (a - behind + A) % A, minor)
        return remote(ref, ref, wx_s.at[n, behind, j], wx_r.at[n, behind, j], dp_dev(a, near(j)))

    def w_send_x(n, behind):
        repeat(1, B, lambda j: wx(n, behind, j, b).start())

    def w_arrive(n, hop):
        @pl.when(a >= hop)
        def _():
            wz(n, 0, hop, a - hop).wait_recv()
            if hop < A - 1:
                pl.when(a < A - 1)(lambda: wz(n, 0, hop + 1, a - hop).start())
            w_send_x(n, hop)

        @pl.when(a + hop < A)
        def _():
            wz(n, 1, hop, a + hop).wait_recv()
            if hop < A - 1:
                pl.when(a > 0)(lambda: wz(n, 1, hop + 1, a + hop).start())
            w_send_x(n, A - hop)

    progress = {"wave": 0, "line": 0, "own": 0, "load": 0}

    def w_wave():
        wave = progress["wave"]
        for n in range(progress["line"], min(wave + 3, len(order))):
            l, g = order[n]
            first = groups[g][0]
            for at, (_, place, wide) in enumerate(weights):
                if first <= place < first + groups[g][1]:
                    loads[l, at].wait()
            pl.when(a < A - 1)(lambda: wz(n, 0, 1, a).start())
            pl.when(a > 0)(lambda: wz(n, 1, 1, a).start())
            progress["line"] = n + 1
        for n in range(progress["own"], min(wave + 6, progress["line"] + 3, len(order))):
            if n < progress["line"]:
                w_send_x(n, 0)
                progress["own"] = n + 1
        for hop in range(1, A):
            if 0 <= wave - hop + 1 < len(order):
                w_arrive(wave - hop + 1, hop)
        progress["wave"] = wave + 1

    def w_pass(l, name, count=4, parts=4):
        chosen = part(sets[name], 0, count, parts)
        if chosen:
            while progress["wave"] < order.index((l, chosen[-1])) + A - 1:
                w_wave()

    def w_done(l, name):
        def one(n, behind):
            repeat(1, B, lambda j: wx(n, behind, j, (b - j + B) % B).wait_recv())

        for g in sets[name]:
            repeat(0, A, functools.partial(one, order.index((l, g))))

    def w_sent(l, g):
        n = order.index((l, g))
        pl.when(a < A - 1)(lambda: wz(n, 0, 1, a).wait_send())
        pl.when(a > 0)(lambda: wz(n, 1, 1, a).wait_send())
        for hop in range(1, A - 1):
            pl.when((a >= hop) & (a < A - 1))(lambda: wz(n, 0, hop + 1, a - hop).wait_send())
            pl.when((a + hop < A) & (a > 0))(lambda: wz(n, 1, hop + 1, a + hop).wait_send())

        def one(behind):
            repeat(1, B, lambda j: wx(n, behind, j, b).wait_send())

        repeat(0, A, one)

    def ag_copy(buf, h, kind, early=0):
        row = hrow(flip(2), h) if kind == 2 else hrow(t, h)
        send, recv = ag_s.at[early, h, kind], ag_r.at[early, h, kind]
        return remote(buf.at[row], buf.at[row], send, recv, ypeer if kind == 0 else sib)

    def ag_arrival(buf, h, kind, early=0):
        row = hrow(flip((2, 1, 3)[kind]), h)
        send, recv = ag_s.at[early, h, kind], ag_r.at[early, h, kind]
        return remote(buf.at[row], buf.at[row], send, recv, ypeer if kind == 0 else sib)

    def ag_start(buf, h, early=0):
        ag_copy(buf, h, 0, early).start()
        ag_copy(buf, h, 1, early).start()

    def ag_near(buf, h, early=0):
        ag_arrival(buf, h, 1, early).wait_recv()

    def ag_far(buf, h, early=0):
        ag_arrival(buf, h, 0, early).wait_recv()
        ag_copy(buf, h, 2, early).start()
        ag_arrival(buf, h, 2, early).wait_recv()
        for kind in range(3):
            ag_copy(buf, h, kind, early).wait_send()

    def rs_copy(h, kind):
        row = own_half(h)
        src, dst = ((SA, RA), (SB, RB), (SC, RC))[kind]
        return remote(src.at[row], dst.at[row], rs_s.at[h, kind], rs_r.at[h, kind], ypeer if kind == 1 else sib)

    def rs_first(h):
        SA[own_half(h), :] = PBUF[0:half, :].astype(bf16)
        rs_copy(h, 0).start()

    def rs_mid(h, term):
        rs_copy(h, 0).wait_recv()
        SB[own_half(h), :] = (term + RA[own_half(h), :].astype(f32)).astype(bf16)
        rs_copy(h, 1).start()

    def rs_second(h):
        SC[own_half(h), :] = PBUF[0:half, :].astype(bf16)
        rs_copy(h, 2).start()
        ACC[own_half(h), :] = PBUF[half:R, :]

    def rs_run(part, hooks={}):
        @pl.loop(0, 4)
        def _(step):
            h = step // 2
            for place, hook in hooks.items():
                pl.when(step == place)(hook)
            PBUF[...] = part(pair(step % 2, h))

            @pl.when(step % 2 == 0)
            def _():
                rs_first(h)
                ACC[own_half(h), :] = PBUF[half:R, :]

            @pl.when(step % 2 == 1)
            def _():
                rs_mid(h, ACC[own_half(h), :])
                rs_second(h)

    def rs_wait(h):
        rs_copy(h, 2).wait_recv()
        rs_copy(h, 1).wait_recv()

    def rs_sum(row):
        return ACC[row, :] + RB[row, :].astype(f32) + RC[row, :].astype(f32)

    def rs_end(h):
        for kind in range(3):
            rs_copy(h, kind).wait_send()

    def by_chunk(h, body):
        @pl.loop(0, half // CHUNK)
        def _(index):
            first = h * half + index * CHUNK
            body(pl.ds(pl.multiple_of(first, CHUNK), CHUNK), pl.ds(pl.multiple_of(t * R + first, CHUNK), CHUNK))

    def head_mask(h):
        lane = lax.broadcasted_iota(jnp.int32, (R, HC), 1)
        return (lane >= h * HD) & (lane < (h + 1) * HD)

    def gsrc(l, first):
        if l == 1:
            return W, 0, first
        if first >= spans["down"][0]:
            return ACT, 1, first - spans["down"][0]
        if first >= spans["up"][0]:
            return GP, 1, first - spans["up"][0]
        return NF2, 1, first

    def gref(l, g, aa, bb):
        first, width = groups[g]
        buf, slot, place = gsrc(l, first)
        return buf.at[slot, shard(aa, bb), pl.ds(place, width)]

    def gb(l, g, j, aa):
        first, width = groups[g]
        return remote(
            gref(l, g, aa, near(j)), BR.at[j - 1, aa, :, pl.ds(first, width)], gb_s.at[l, g, j, aa], gb_r.at[l, g, j, aa],
            dp_dev(a, near(j)),
        )

    def ga(l, g, k):
        first, width = groups[g]
        return remote(
            gref(l, g, far(k), b), AR.at[k - 1, :, pl.ds(first, width)], ga_s.at[l, g, k], ga_r.at[l, g, k], dp_dev(far(k), b)
        )

    def g_start(l, g):
        if l == 0:
            pl.semaphore_wait(cred_b.at[g], B - 1)

        def one(k):
            repeat(1, B, lambda j: gb(l, g, j, far(k)).start())

        repeat(1, A + 1, one)

    def g_piece(l, g, aa):
        first, width = groups[g]
        repeat(1, B, lambda j: gb(l, g, j, aa).wait_recv())
        total = gref(l, g, aa, b)[...].astype(f32)
        for j in range(1, B):
            total = total + BR[j - 1, aa, :, first : first + width].astype(f32)
        return total

    def g_far(l, g, k):
        piece = gref(l, g, far(k), b)
        piece[...] = g_piece(l, g, far(k)).astype(bf16)
        ga(l, g, k).start()

    def g_own(l, g):
        first, width = groups[g]
        OST[l, :, first : first + width] = g_piece(l, g, a)
        if l == 1:
            repeat(
                1, B,
                lambda j: pl.semaphore_signal(cred_b.at[g], inc=1, device_id=dp_dev(a, near(j)), device_id_type=MESH),
            )

    pieces = [(l, g, k) for l in (1, 0) for name in ("down", "up", "qkv", "out") for g in sets[name] for k in range(1, A + 1)]
    passed = {"count": 0}

    def g_upto(point):
        due = -(-SCHEDULE[point] * len(pieces) // 96)
        for l, g, k in pieces[passed["count"] : due]:
            if l == 0 and k == 1:
                pl.semaphore_wait(cred_a.at[g], A - 1)
            if k == A:
                g_own(l, g)
            else:
                g_far(l, g, k)
        passed["count"] = max(due, passed["count"])

    def g_out(l, name):
        first, width = spans[name]
        return [
            pltpu.make_async_copy(OST.at[l, :, pl.ds(place, wide)], dst.at[l], loc.at[l, at])
            for at, (dst, place, wide) in enumerate(
                ((gq, 0, HC), (gk, HC, HC), (gv, 2 * HC, HC), (go, 3 * HC, HC), (gu, 4 * HC, FC), (gd, 4 * HC + FC, FC))
            )
            if first <= place < first + width
        ]

    def g_final(l, name):
        for g in sets[name]:
            first, width = groups[g]

            def one(k):
                ga(l, g, k).wait_recv()
                OST[l, :, first : first + width] += AR[k - 1, :, first : first + width].astype(f32)

            repeat(1, A, one)
            if l == 1:
                repeat(
                    1, A,
                    lambda k: pl.semaphore_signal(cred_a.at[g], inc=1, device_id=dp_dev(far(k), b), device_id_type=MESH),
                )
        for copy in g_out(l, name):
            copy.start()

    def g_sent(l, g):
        repeat(1, A, lambda k: ga(l, g, k).wait_send())

        def one(k):
            repeat(1, B, lambda j: gb(l, g, j, far(k)).wait_send())

        repeat(1, A + 1, one)

    def weight_grad(l, name, left, right):
        first, width = spans[name]
        buf, slot, place = gsrc(l, first)

        @pl.loop(0, D // R)
        def _(i):
            buf[slot, blk(i), place : place + width] = dot_tn(left[:, blk(i)], right[...]).astype(bf16)

        for g in sets[name]:
            g_start(l, g)

    def reload(at):
        first, width = tuple(spans.values())[at]
        return pltpu.make_async_copy(spill.at[:, pl.ds(first, width)], W.at[1, :, pl.ds(first, width)], loc.at[1, 6 + at])

    def vgx(l, j):
        return remote(vg.at[l], VGX.at[l, j - 1], vgx_s.at[l, j], vgx_r.at[l, j], dp_dev(a, near(j)))

    def vgz(l, k):
        return remote(VGS.at[l], VGZ.at[l, k - 1], vgz_s.at[l, k], vgz_r.at[l, k], dp_dev(far(k), b))

    def vgt(l, i):
        return remote(VGU.at[l], VGT.at[l, i - 1], vgt_s.at[l, i], vgt_r.at[l, i], (dp, flip(i)))

    def vg_near(l):
        repeat(1, B, lambda j: vgx(l, j).start())

    def vg_far(l):
        repeat(1, B, lambda j: vgx(l, j).wait_recv())
        VGS[l] = vg[l]
        for j in range(1, B):
            VGS[l] += VGX[l, j - 1]
        repeat(1, A, lambda k: vgz(l, k).start())

    def vg_tensor(l):
        repeat(1, A, lambda k: vgz(l, k).wait_recv())
        VGU[l] = VGS[l]
        for k in range(1, A):
            VGU[l] += VGZ[l, k - 1]
        repeat(1, 4, lambda i: vgt(l, i).start())

    def own_lanes(ref, start):
        if S % 128 == 0:
            return ref[:, pl.ds(pl.multiple_of(start, 128), S)]
        tile = ref[:, pl.ds(pl.multiple_of(start // 128 * 128, 128), 128)]
        return pltpu.roll(tile, (128 - start % 128) % 128, 1)[:, 0:S]

    def vg_end(l):
        repeat(1, 4, lambda i: vgt(l, i).wait_recv())
        owner = dp // quarter
        total = VGU[l]
        picked = jnp.where(flip(0) == owner, VGU[l], 0.0)
        for i in range(1, 4):
            total = total + VGT[l, i - 1]
            picked = picked + jnp.where(flip(i) == owner, VGT[l, i - 1], 0.0)
        TOT[0:8, :] = total
        TOT[8:16, :] = picked
        inside = dp % quarter
        VS[l, 0:6, 0:S] = own_lanes(TOT.at[0:8], dp * S)[0:6, :]
        VS[l, 6:7, 0:S] = own_lanes(TOT.at[8:16], inside * S)[7:8, :]
        VS[l, 7:8, 0:S] = own_lanes(TOT.at[8:16], HC + inside * S)[7:8, :]
        for q in range(4):
            VS[l, 8 + q : 9 + q, 0:S] = own_lanes(TOT.at[8:16], inside * 4 * S + q * S)[6:7, :]
        repeat(1, B, lambda j: vgx(l, j).wait_send())
        repeat(1, A, lambda k: vgz(l, k).wait_send())
        repeat(1, 4, lambda i: vgt(l, i).wait_send())

    def low_grad(l, row, full, grad):
        GC[row, :] = grad
        low = grad.astype(bf16)
        GF[full, :] = low
        vg[l, 5:6, :] += jnp.sum(low.astype(f32), axis=0, keepdims=True)

    def pre_back(l, rows):
        act_grad = dot_nn(both(GF, rows), W[1, :, 4 * HC + FC : 4 * HC + 2 * FC])
        pre_grad = (act_grad * both(GP.at[l], rows).astype(f32)).astype(bf16)
        put(GP.at[l], rows, pre_grad)
        vg[l, 6:7, :] += jnp.sum(pre_grad.astype(f32), axis=0, keepdims=True)
        return pre_grad

    def norm_back(l, place, dy, rows, gain):
        n, scale = norm_parts(rows)
        vg[l, place : place + 1, :] += jnp.sum(dy * n, axis=0, keepdims=True)
        vg[l, place + 1 : place + 2, :] += jnp.sum(dy, axis=0, keepdims=True)
        dn = dy * gain
        return scale * (dn - jnp.mean(dn, axis=-1, keepdims=True) - n * jnp.mean(dn * n, axis=-1, keepdims=True))

    def vz(k, source, device):
        ref = RAW.at[source * B + b]
        return remote(ref, ref, vz_s.at[k], vz_r.at[k], device)

    def vx(k, j, minor, device):
        ref = RAW.at[(a - k + A) % A * B + minor]
        return remote(ref, ref, vx_s.at[k, j], vx_r.at[k, j], device)

    def v_send_x(k):
        repeat(1, B, lambda j: vx(k, j, b, dp_dev(a, near(j))).start())

    def v_pass(k):
        vz(k, (a - k + A) % A, dp_dev(far(k), b)).wait_recv()
        v_send_x(k)

    def v_done(k):
        repeat(1, B, lambda j: vx(k, j, (b - j + B) % B, dp_dev(a, near(j))).wait_recv())

    def v_sent(k):
        repeat(1, B, lambda j: vx(k, j, b, dp_dev(a, near(j))).wait_send())

    repeat(1, A, lambda k: vz(k, a, dp_dev(far(k), b)).start())
    v_send_x(0)

    w_wave()
    tok_copy.wait()
    repeat(1, A, v_pass)
    repeat(0, A, v_done)
    repeat(1, A, lambda k: vz(k, a, dp_dev(far(k), b)).wait_send())
    repeat(0, A, v_sent)

    def lay_out(row, offset, pieces):
        per_tile = max(1, 128 // S)
        for start in range(0, len(pieces), per_tile):
            run = pieces[start : start + per_tile]
            value = run[0] if len(run) == 1 else jnp.concatenate([piece[:, 0:S] for piece in run], axis=1)
            at = offset + start * S
            vec[row[0], row[1] : row[1] + 1, at : at + len(run) * S] = value[:, 0 : len(run) * S]

    for l in range(2):
        for place in range(6):
            lay_out((l, place), 0, [RAW[d, 12 * l + place : 12 * l + place + 1, :] for d in range(A * B)])
        for place in range(2):
            lay_out(
                (l, 7), place * HC,
                [RAW[t * quarter + d, 12 * l + 6 + place : 12 * l + 7 + place, :] for d in range(quarter)],
            )
        lay_out(
            (l, 6), 0,
            [RAW[t * quarter + d, 12 * l + 8 + q : 12 * l + 9 + q, :] for d in range(quarter) for q in range(4)],
        )

    spills = [
        pltpu.make_async_copy(W.at[0, :, pl.ds(first, width)], spill.at[:, pl.ds(first, width)], loc.at[1, 6 + at])
        for at, (first, width) in enumerate(spans.values())
    ]

    def first_norm(l, row, full):
        n, _ = norm_parts(X[l, row, :])
        NF[l, full, :] = (n * vec[l, 0:1, :] + vec[l, 1:2, :]).astype(bf16)

    @pl.loop(0, 2)
    def _(h):
        def one(row, full):
            X[0, row, :] = STB[row, :].astype(f32)
            first_norm(0, row, full)

        by_chunk(h, one)
        ag_start(NF.at[0], h)

    cot_copy.start()
    cot_copy.wait()

    @pl.loop(0, 2)
    def _(h):
        by_chunk(h, lambda row, full: low_grad(1, row, full, STB[row, :].astype(f32) * live))
        ag_start(GF, h, 1)

    for l in range(2):
        if l == 0:
            w_pass(0, "qkv")
        w_done(l, "qkv")
        w_pass(l, "out")

        def project(rows):
            out = dot_nn(both(NF.at[l], rows), W[l, :, 0 : 3 * HC])
            queries = out[:, 0:HC] + vec[l, 7:8, 0:HC]
            values = out[:, 2 * HC : 3 * HC] + vec[l, 7:8, HC : 2 * HC]
            put(QKV.at[l], rows, jnp.concatenate([queries, out[:, HC : 2 * HC], values], axis=1).astype(bf16))

        @pl.loop(0, 4)
        def _(step):
            h = step % 2
            pl.when(step < 2)(lambda: ag_near(NF.at[l], h))
            pl.when(step >= 2)(lambda: ag_far(NF.at[l], h))
            project(pair(1 - step // 2, h))

        if l == 0:

            @pl.loop(0, 2)
            def _(h):
                ag_near(GF, h, 1)
                ag_far(GF, h, 1)

        TR[...] = QKV[l, :, 2 * HC : 3 * HC].T
        w_done(l, "out")

        def attend(rows):
            queries = both(QKV.at[l, :, pl.ds(0, HC)], rows)
            keys = QKV[l, :, HC : 2 * HC]
            outs = []
            for h in range(heads):
                masked = jnp.where(head_mask(h), queries, jnp.zeros_like(queries))
                scores = dot_nt(keys, masked) * (score_scale * LOG2E)
                top = jnp.max(scores, axis=0, keepdims=True)
                exps = jnp.exp2(scores - top)
                total = jnp.sum(exps, axis=0, keepdims=True)
                log_sum = top + jnp.log(total) * LOG2E
                LSE[l, h : h + 1, rows[0]] = log_sum[:, 0:half]
                LSE[l, h : h + 1, rows[1]] = log_sum[:, half:R]
                outs.append(dot_nn(TR[h * HD : (h + 1) * HD, :], exps.astype(bf16)) * (1.0 / total))
            attended = jnp.concatenate(outs, axis=0).T.astype(bf16)
            put(AT.at[l], rows, attended)
            return dot_nt(attended, W[l, :, 3 * HC : 4 * HC])

        rs_run(
            attend,
            {1: lambda: w_pass(l, "up", 1), 2: lambda: w_pass(l, "up", 2), 3: lambda: w_pass(l, "up", 3)},
        )

        @pl.loop(0, 2)
        def _(h):
            pl.when(h == 1)(lambda: w_pass(l, "up"))
            rs_wait(h)

            def second_norm(row, full):
                middle = X[l, row, :] + rs_sum(row) + vec[l, 2:3, :]
                MID[l, row, :] = middle
                n, _ = norm_parts(middle)
                NF2[l, full, :] = (n * vec[l, 3:4, :] + vec[l, 4:5, :]).astype(bf16)

            by_chunk(h, second_norm)
            rs_end(h)
            ag_start(NF2.at[l], h)

        w_done(l, "up")

        @pl.loop(0, 4)
        def _(step):
            h = step % 2
            pl.when(step == 0)(lambda: w_pass(l, "down", 1))
            pl.when(step == 2)(lambda: w_pass(l, "down", 2))
            pl.when(step == 3)(lambda: w_pass(l, "down", 3))
            pl.when(step < 2)(lambda: ag_near(NF2.at[l], h))
            pl.when(step >= 2)(lambda: ag_far(NF2.at[l], h))
            rows = pair(1 - step // 2, h)
            pre = dot_nn(both(NF2.at[l], rows), W[l, :, 4 * HC : 4 * HC + FC]) + vec[l, 6:7, :]
            cumul = 0.5 * (1.0 + lax.erf(pre * ROOT_HALF))
            put(ACT.at[l], rows, (pre * cumul).astype(bf16))
            put(GP.at[l], rows, (cumul + pre * (jnp.exp(-0.5 * pre * pre) * PHI_ZERO)).astype(bf16))

        if l == 1:
            w_pass(1, "down", 3)
            for copy in spills:
                copy.wait()
            weight_grad(1, "down", GF, ACT.at[1])
        w_pass(l, "down")
        w_done(l, "down")

        def feed_out(rows):
            return dot_nt(both(ACT.at[l], rows), W[l, :, 4 * HC + FC : 4 * HC + 2 * FC])

        if l == 0:
            rs_run(feed_out, {2: lambda: w_pass(1, "qkv", 1, 3)})
            w_pass(1, "qkv", 2, 3)

            @pl.loop(0, 2)
            def _(h):
                pl.when(h == 1)(lambda: w_pass(1, "qkv"))
                rs_wait(h)

                def layer_out(row, full):
                    X[1, row, :] = MID[0, row, :] + rs_sum(row) + vec[0, 5:6, :]
                    first_norm(1, row, full)

                by_chunk(h, layer_out)
                rs_end(h)
                ag_start(NF.at[1], h)

        else:

            @pl.loop(0, 4)
            def _(step):
                pre_back(1, pair(step % 2, step // 2))

            rs_run(lambda rows: dot_nt(both(GP.at[1], rows), W[1, :, 4 * HC : 4 * HC + FC]))
            weight_grad(1, "up", NF2.at[1], GP.at[1])
            g_upto(0)

        if l == 0:
            for g in range(len(groups)):
                w_sent(0, g)
            for copy in spills:
                copy.start()

    def last_out(row, full):
        STB[row, :] = (MID[1, row, :] + rs_sum(row) + vec[1, 5:6, :]).astype(bf16)

    def greet_pairs():
        for device in (sib, ypeer):
            pl.semaphore_signal(ack, inc=1, device_id=device, device_id_type=MESH)
        pl.semaphore_wait(ack, 2)

    for l in (1, 0):
        if l == 0:
            reload(3).wait()
            reload(2).wait()

        if l == 0:

            def feed_back(rows):
                PBUF[...] = dot_nt(pre_back(0, rows), W[1, :, 4 * HC : 4 * HC + FC])

            @pl.loop(0, 2)
            def _(h):
                ag_near(GF, h)
                feed_back(near_pair(h))
                rs_second(h)

            g_upto(9)


            @pl.loop(0, 2)
            def _(h):
                @pl.when(h == 1)
                def _():
                    rs_mid(0, PBUF[half:R, :])
                    g_upto(10)

                ag_far(GF, h)
                feed_back(far_pair(h))
                rs_first(h)

            rs_mid(1, PBUF[half:R, :])
            g_upto(11)
            vg_far(1)
            g_final(1, "down")
            weight_grad(0, "down", GF, ACT.at[0])
            g_upto(12)

        @pl.loop(0, 2)
        def _(h):
            rs_wait(h)

            def second_back(row, full):
                grad = GC[row, :] + norm_back(l, 3, rs_sum(row), MID[l, row, :], vec[l, 3:4, :])
                GC[row, :] = grad
                low = grad.astype(bf16)
                MF[full, :] = low
                vg[l, 2:3, :] += jnp.sum(low.astype(f32), axis=0, keepdims=True)

            by_chunk(h, second_back)
            rs_end(h)
            ag_start(MF, h)

            @pl.when(h == 0)
            def _():
                if l == 0:
                    weight_grad(0, "up", NF2.at[0], GP.at[0])
                g_upto(2 if l == 1 else 13)

        if l == 0:
            vg_tensor(1)
            g_final(1, "up")
            g_upto(14)
            reload(1).wait()
            reload(0).wait()
        if l == 1:
            greet_pairs()
            rs_run(feed_out)
            g_upto(1)
        TR[...] = QKV[l, :, HC : 2 * HC].T
        DKA[...] = jnp.zeros_like(DKA)
        PBUF[...] = jnp.zeros_like(PBUF)

        @pl.loop(0, 4)
        def _(step):
            h = step % 2
            for place in (1, 2, 3):
                pl.when(step == place)(lambda: g_upto(place + (2 if l == 1 else 14)))
            pl.when(step < 2)(lambda: ag_near(MF, h))
            pl.when(step >= 2)(lambda: ag_far(MF, h))
            rows = pair(1 - step // 2, h)
            out_grads = dot_nn(both(MF, rows), W[1, :, 3 * HC : 4 * HC]).astype(bf16)
            queries = both(QKV.at[l, :, pl.ds(0, HC)], rows)
            keys = QKV[l, :, HC : 2 * HC]
            values = QKV[l, :, 2 * HC : 3 * HC]
            parts = []
            for head in range(heads):
                mask = head_mask(head)
                q_one = jnp.where(mask, queries, jnp.zeros_like(queries))
                do_one = jnp.where(mask, out_grads, jnp.zeros_like(out_grads))
                log_sum = jnp.concatenate([LSE[l, head : head + 1, rows[0]], LSE[l, head : head + 1, rows[1]]], axis=1)
                probs = jnp.exp2(dot_nt(keys, q_one) * (score_scale * LOG2E) - log_sum)
                prob_grad = dot_nt(values, do_one)
                value_part = dot_nn(probs.astype(bf16), do_one)
                for place in range(4):
                    PBUF[:, place * HC : (place + 1) * HC] += value_part[place * R : (place + 1) * R, :]
                row_dot = jnp.sum(probs * prob_grad, axis=0, keepdims=True)
                score_grad = (probs * (prob_grad - row_dot)).astype(bf16)
                DKA[...] += dot_nn(score_grad, q_one)
                parts.append(dot_nn(TR[head * HD : (head + 1) * HD, :], score_grad))
            query_low = (jnp.concatenate(parts, axis=0).T * score_scale).astype(bf16)
            put(DQKV.at[:, pl.ds(0, HC)], rows, query_low)

        g_upto(6 if l == 1 else 18)
        DQKV[:, HC : 2 * HC] = (DKA[...] * score_scale).astype(bf16)
        for place in range(4):
            DQKV[place * R : (place + 1) * R, 2 * HC : 3 * HC] = PBUF[:, place * HC : (place + 1) * HC].astype(bf16)
        weight_grad(l, "qkv", NF.at[l], DQKV)
        if l == 1:
            for g in range(len(groups)):
                w_sent(1, g)
            for at in (1, 2, 3):
                reload(at).start()

            @pl.loop(0, 2)
            def _(h):
                rs_wait(h)
                by_chunk(h, last_out)
                rs_end(h)

            mixed_copy = pltpu.make_async_copy(STB, mixed.at[0], loc.at[0, 6])
            mixed_copy.start()
            greet_pairs()
        g_upto(7 if l == 1 else 19)
        rs_run(lambda rows: dot_nt(both(DQKV, rows), W[1, :, 0 : 3 * HC]))
        if l == 1:
            reload(0).start()
        weight_grad(l, "out", MF, AT.at[l])
        vg[l, 7:8, 0:HC] = jnp.sum(DQKV[:, 0:HC].astype(f32), axis=0, keepdims=True)
        vg[l, 7:8, HC : 2 * HC] = jnp.sum(DQKV[:, 2 * HC : 3 * HC].astype(f32), axis=0, keepdims=True)
        g_upto(24 if l == 1 else 25)
        if l == 0:
            vg_end(1)

        @pl.loop(0, 2)
        def _(h):
            rs_wait(h)

            def first_back(row, full):
                grad = GC[row, :] + norm_back(l, 0, rs_sum(row), X[l, row, :], vec[l, 0:1, :])
                if l == 1:
                    low_grad(0, row, full, grad)
                else:
                    GC[row, :] = grad

            by_chunk(h, first_back)
            rs_end(h)
            if l == 1:
                ag_start(GF, h)

        vg_near(l)
        if l == 1:
            g_upto(8)

    mixed_copy.wait()
    grad_copy = pltpu.make_async_copy(GC, tgrad.at[0], loc.at[0, 7])
    grad_copy.start()
    g_upto(20)
    vg_far(0)
    g_final(1, "qkv")
    g_final(1, "out")
    g_upto(21)
    g_final(0, "down")
    vg_tensor(0)
    g_upto(22)
    vg_end(0)
    g_final(0, "up")
    g_upto(23)
    g_final(0, "qkv")
    vs_copy = pltpu.make_async_copy(VS, vs_out, loc.at[0, 6])
    vs_copy.start()
    g_final(0, "out")
    grad_copy.wait()
    vs_copy.wait()
    for l in range(2):
        for g in range(len(groups)):
            g_sent(l, g)
        for name in spans:
            for copy in g_out(l, name):
                copy.wait()


def finish_kernel(S, *refs):
    sources, small, targets, smalls, stages, sems = refs[:8], refs[8], refs[9:17], refs[17:26], refs[26:34], refs[34]
    arrivals = [
        pltpu.make_async_copy(source, stage, sems.at[0, at]) for at, (source, stage) in enumerate(zip(sources, stages))
    ]
    copies = [
        pltpu.make_async_copy(stage, target, sems.at[1, at]) for at, (stage, target) in enumerate(zip(stages, targets))
    ]
    for arrival in arrivals:
        arrival.start()
    for arrival, copy in zip(arrivals, copies):
        arrival.wait()
        copy.start()
    for l in range(2):
        for place in range(8):
            smalls[place][l : l + 1, :] = small[l, place : place + 1, 0:S]
        for q in range(4):
            smalls[8][l : l + 1, q * S : (q + 1) * S] = small[l, 8 + q : 9 + q, 0:S]
    for copy in copies:
        copy.wait()


def shards(
    mesh_dp,
    tokens, clip_counts, cotangent, norm1_gain, norm1_shift, w_query, query_bias, w_key, w_value, value_bias, w_out,
    out_bias, norm2_gain, norm2_shift, w_up, up_bias, w_down, down_bias,
):
    layers, S, HC = w_query.shape
    FC = w_up.shape[2]
    _, R, D = tokens.shape
    B = 1
    while 4 * B * B <= mesh_dp:
        B *= 2
    A = mesh_dp // B
    LEN = 4 * R
    COLS = 4 * HC + 2 * FC
    dims = (A, B, S, R, D, HC, FC)
    parts = COLS // HC if A * B <= 16 else 4
    vm = pltpu.VMEM
    dma = pltpu.SemaphoreType.DMA
    any_spec = pl.BlockSpec(memory_space=pl.ANY)
    vmem_spec = pl.BlockSpec(memory_space=pltpu.VMEM)
    grad_small = jax.ShapeDtypeStruct((layers, S, HC), f32)
    grad_large = jax.ShapeDtypeStruct((layers, S, FC), f32)
    outs = pl.pallas_call(
        functools.partial(encoder_kernel, dims),
        out_shape=(
            jax.ShapeDtypeStruct((1, R, D), bf16),
            jax.ShapeDtypeStruct((1, R, D), f32),
            grad_small, grad_small, grad_small, grad_small, grad_large, grad_large,
            jax.ShapeDtypeStruct((layers, 16, 128), f32),
            jax.ShapeDtypeStruct((D, COLS), bf16),
        ),
        in_specs=[any_spec, any_spec, pl.BlockSpec(memory_space=pltpu.SMEM)] + [any_spec] * 6 + [vmem_spec] * 9,
        out_specs=tuple([any_spec] * 10),
        scratch_shapes=[
            vm((2, D, COLS), bf16),
            vm((2, LEN, D), bf16),
            vm((2, LEN, 3 * HC), bf16),
            vm((2, LEN, HC), bf16),
            vm((2, 8, LEN), f32),
            vm((2, R, D), f32),
            vm((2, R, D), f32),
            vm((2, LEN, D), bf16),
            vm((2, LEN, FC), bf16),
            vm((2, LEN, FC), bf16),
            vm((LEN, D), bf16),
            vm((LEN, D), bf16),
            vm((LEN, 3 * HC), bf16),
            vm((R, D), f32),
            vm((max(B - 1, 1), A, S, COLS), bf16),
            vm((max(A - 1, 1), S, COLS), bf16),
            vm((R, D), bf16), vm((R, D), bf16), vm((R, D), bf16),
            vm((R, D), bf16), vm((R, D), bf16), vm((R, D), bf16),
            vm((R, D), f32), vm((R, D), f32),
            vm((2, S, COLS), f32),
            vm((HC, LEN), bf16),
            vm((LEN, HC), f32),
            vm((R, D), bf16),
            vm((A * B, 24, 128), f32),
            vm((2, 8, D), f32), vm((2, 8, D), f32),
            vm((2, max(B - 1, 1), 8, D), f32),
            vm((2, 8, D), f32),
            vm((2, max(A - 1, 1), 8, D), f32),
            vm((2, 8, D), f32),
            vm((2, 3, 8, D), f32),
            vm((2, 16, 128), f32),
            vm((16, D), f32),
            dma((2, 10)),
            dma((2, 2, 3)), dma((2, 2, 3)), dma((2, 3)), dma((2, 3)),
            dma((2 * parts, 2, A)), dma((2 * parts, 2, A)), dma((2 * parts, A, B)), dma((2 * parts, A, B)),
            dma((2, parts, B, A)), dma((2, parts, B, A)), dma((2, parts, A)), dma((2, parts, A)),
            dma((A,)), dma((A,)), dma((A, B)), dma((A, B)),
            dma((2, B)), dma((2, B)), dma((2, A)), dma((2, A)), dma((2, 4)), dma((2, 4)),
            pltpu.SemaphoreType.REGULAR((parts,)), pltpu.SemaphoreType.REGULAR((parts,)), pltpu.SemaphoreType.REGULAR,
        ],
        compiler_params=pltpu.CompilerParams(
            collective_id=0, has_side_effects=True, vmem_limit_bytes=64 * 2**20 - 2**17
        ),
        name="encoder",
    )(tokens, cotangent, clip_counts, w_query, w_key, w_value, w_out, w_up, w_down, norm1_gain, norm1_shift,
      out_bias, norm2_gain, norm2_shift, down_bias, query_bias, value_bias, up_bias)

    small = jax.ShapeDtypeStruct((layers, S), f32)
    large_types = tuple(jax.ShapeDtypeStruct(member.shape, member.dtype) for member in outs[:8])
    (mixed, tokens_grad, gq, gk, gv, go, gu, gd, g_gain_one, g_shift_one, g_out, g_gain_two, g_shift_two, g_down, g_query,
     g_value, g_up) = pl.pallas_call(
        functools.partial(finish_kernel, S),
        out_shape=large_types + (small,) * 8 + (jax.ShapeDtypeStruct((layers, 4 * S), f32),),
        in_specs=[any_spec] * 8 + [vmem_spec],
        out_specs=tuple([any_spec] * 8 + [vmem_spec] * 9),
        scratch_shapes=[vm(member.shape, member.dtype) for member in outs[:8]] + [dma((2, 8))],
        compiler_params=pltpu.CompilerParams(vmem_limit_bytes=64 * 2**20 - 2**17),
        name="finish",
    )(*outs[:9])
    return (
        mixed, tokens_grad, g_gain_one, g_shift_one, gq, g_query, gk, gv, g_value, go, g_out, g_gain_two, g_shift_two, gu,
        g_up, gd, g_down,
    )


def solution(mesh):
    rows = P("dp", "tensor", None)
    vector = P(None, "dp")
    matrix = P(None, "dp", "tensor")
    return jax.shard_map(
        functools.partial(shards, mesh.shape["dp"]),
        mesh=mesh,
        in_specs=(
            rows, P("dp"), rows, vector, vector, matrix, vector, matrix, matrix, vector, matrix, vector, vector, vector,
            matrix, vector, matrix, vector,
        ),
        out_specs=(
            rows, rows, vector, vector, matrix, vector, matrix, matrix, vector, matrix, vector, vector, vector, matrix,
            vector, matrix, vector,
        ),
        check_vma=False,
    )
```

time: 418 us -> 400 us (0.957)
  Pallas kernels: 413 us -> 392 us
    pallas_call x1, Pallas kernels: 408 us -> 386 us  [shards(): pl.pallas_call(functools.partial(encoder_kernel, dims), out_shape=(jax.Sh...]
where the time goes in v3:
time: 400 us; the launch traced here: 393 us
  Pallas kernels  392 us (98%)
    pallas_call x1, Pallas kernels, shards(): pl.pallas_call(functools.partial(encoder_kernel, dims), out_shape=(jax.Sh...  386 us

profile of v3, /device:TPU:0, one launch (start us, length us, event | category | flops | bytes accessed | tf_op | source)
XLA Modules:
  0.0 393.4 jit_solution(9121189741372112001)
XLA Ops:
  1.3 386.1 %encoder.1 = (bf16[1,256,1024]{2,1,0:T(8,128)(2,1)}, f32[1,256,1024]{2,1,0:T(8,128)}, f32[2,128,256]{2,1,0:T(8,128)}, f32[2,128,256]{2,1,0:T(8,128)}, f32[2,128,...) custom-call(bf16[1,256,1024]{2,1,0:T(8,128)(2,1)} %tok.1, ...), custom_call_target="tpu_custom_call" | custom-call | tf_op jit(solution)/shard_map/encoder/pallas_call | solution.py:960
  387.4 5.5 %finish.1 = (bf16[1,256,1024]{2,1,0:T(8,128)(2,1)}, f32[1,256,1024]{2,1,0:T(8,128)}, f32[2,128,256]{2,1,0:T(8,128)}, f32[2,128,256]{2,1,0:T(8,128)}, f32[2,128,2...) custom-call(bf16[1,256,1024]{2,1,0:T(8,128)(2,1)} %get-tuple-element, ...), custom_call_target="tpu_custom_call" | custom-call | tf_op jit(solution)/shard_map/finish/pallas_call | solution.py:1022

commit v4 on v3

--- a/solution.py
+++ b/solution.py
@@ -17,7 +17,7 @@
 PHI_ZERO = 1.0 / math.sqrt(2.0 * math.pi)
 LOG2E = 1.0 / math.log(2.0)
 CHUNK = 64
-SCHEDULE = (0, 16, 4, 16, 20, 20, 24, 28, 36, 40, 44, 48, 48, 52, 52, 56, 60, 60, 64, 64, 76, 80, 92, 96, 32, 72)
+SCHEDULE = (4, 18, 10, 22, 26, 30, 32, 32, 44, 48, 48, 48, 48, 56, 60, 64, 64, 68, 72, 76, 80, 88, 96, 96, 40, 80, 14)
 
 
 def dot_nn(left, right):
@@ -387,7 +387,10 @@
     passed = {"count": 0}
 
     def g_upto(point):
-        due = -(-SCHEDULE[point] * len(pieces) // 96)
+        left, due = SCHEDULE[point], 0
+        for name, size in 2 * (("down", 16), ("up", 16), ("qkv", 12), ("out", 4)):
+            due += min(left, size) * len(sets[name]) * A // size
+            left = max(left - size, 0)
         for l, g, k in pieces[passed["count"] : due]:
             if l == 0 and k == 1:
                 pl.semaphore_wait(cred_a.at[g], A - 1)
@@ -763,10 +766,10 @@
                 rs_first(h)
 
             rs_mid(1, PBUF[half:R, :])
+            weight_grad(0, "down", GF, ACT.at[0])
             g_upto(11)
             vg_far(1)
             g_final(1, "down")
-            weight_grad(0, "down", GF, ACT.at[0])
             g_upto(12)
 
         @pl.loop(0, 2)
@@ -797,6 +800,7 @@
             reload(1).wait()
             reload(0).wait()
         if l == 1:
+            g_upto(26)
             greet_pairs()
             rs_run(feed_out)
             g_upto(1)
@@ -858,7 +862,8 @@
         rs_run(lambda rows: dot_nt(both(DQKV, rows), W[1, :, 0 : 3 * HC]))
         if l == 1:
             reload(0).start()
-        weight_grad(l, "out", MF, AT.at[l])
+        if l == 1:
+            weight_grad(1, "out", MF, AT.at[1])
         vg[l, 7:8, 0:HC] = jnp.sum(DQKV[:, 0:HC].astype(f32), axis=0, keepdims=True)
         vg[l, 7:8, HC : 2 * HC] = jnp.sum(DQKV[:, 2 * HC : 3 * HC].astype(f32), axis=0, keepdims=True)
         g_upto(24 if l == 1 else 25)
@@ -884,6 +889,8 @@
         vg_near(l)
         if l == 1:
             g_upto(8)
+        else:
+            weight_grad(0, "out", MF, AT.at[0])
 
     mixed_copy.wait()
     grad_copy = pltpu.make_async_copy(GC, tgrad.at[0], loc.at[0, 7])
@@ -893,12 +900,12 @@
     g_final(1, "qkv")
     g_final(1, "out")
     g_upto(21)
-    g_final(0, "down")
     vg_tensor(0)
     g_upto(22)
+    g_upto(23)
+    g_final(0, "down")
+    g_final(0, "up")
     vg_end(0)
-    g_final(0, "up")
-    g_upto(23)
     g_final(0, "qkv")
     vs_copy = pltpu.make_async_copy(VS, vs_out, loc.at[0, 6])
     vs_copy.start()

time: 400 us -> 391 us (0.978)
  Pallas kernels: 392 us -> 383 us
    pallas_call x1, Pallas kernels: 386 us -> 378 us  [shards(): pl.pallas_call(functools.partial(encoder_kernel, dims), out_shape=(jax.Sh...]
where the time goes in v4:
time: 391 us; the launch traced here: 385 us
  Pallas kernels  383 us (98%)
    pallas_call x1, Pallas kernels, shards(): pl.pallas_call(functools.partial(encoder_kernel, dims), out_shape=(jax.Sh...  378 us

profile of v4, /device:TPU:0, one launch (start us, length us, event | category | flops | bytes accessed | tf_op | source)
XLA Modules:
  0.0 384.9 jit_solution(10126755472783095220)
XLA Ops:
  1.3 377.6 %encoder.1 = (bf16[1,256,1024]{2,1,0:T(8,128)(2,1)}, f32[1,256,1024]{2,1,0:T(8,128)}, f32[2,128,256]{2,1,0:T(8,128)}, f32[2,128,256]{2,1,0:T(8,128)}, f32[2,128,...) custom-call(bf16[1,256,1024]{2,1,0:T(8,128)(2,1)} %tok.1, ...), custom_call_target="tpu_custom_call" | custom-call | tf_op jit(solution)/shard_map/encoder/pallas_call | solution.py:967
  378.9 5.5 %finish.1 = (bf16[1,256,1024]{2,1,0:T(8,128)(2,1)}, f32[1,256,1024]{2,1,0:T(8,128)}, f32[2,128,256]{2,1,0:T(8,128)}, f32[2,128,256]{2,1,0:T(8,128)}, f32[2,128,2...) custom-call(bf16[1,256,1024]{2,1,0:T(8,128)(2,1)} %get-tuple-element, ...), custom_call_target="tpu_custom_call" | custom-call | tf_op jit(solution)/shard_map/finish/pallas_call | solution.py:1029
